TPU v7x, 128 devices: a whole 4x4x4 slice. The times are simulated.
128 devices in a mesh: gr: 8 (over y, z_lo), gc: 16 (over z_hi, x, core).
Axes of the slice: x: 4, y: 4, z: 4 (z_hi: 2, z_lo: 2; z = z_hi * 2 + z_lo), core: 2. Of those that a mesh axis runs over, the one named last changes fastest.
Arguments:
- iterate: bfloat16 [3584, 18432], P(('gr', 'gc')), may hold values from -0.3 to 0.3, as said below
Outputs:
- update: bfloat16 [3584, 18432], P(('gr', 'gc'))
Inputs may be any that keep to these rules, and one draw needn't show every extreme that they name: The iterate of earlier Newton-Schulz steps, with singular values of order one.
All inputs are finite; a program needn't handle non-finite values.
Results may differ from a plain program's by a relative error of at most 0.02.
Values may be sent and summed in bfloat16 or wider, within the bound.
No kernel may reach another device: no remote copies, remote signals or barrier semaphores. Data moves between devices by JAX's collectives and lax.ppermute only.
A program may use at most 128 MiB of HBM per device.

v0:
```python
import math

import jax
import jax.numpy as jnp
from jax import lax
from jax.sharding import PartitionSpec as P

M = 3584
N = 18432


LINEAR_COEF = 3.4445
CUBIC_COEF = -4.775
QUINTIC_COEF = 2.0315


def body(iterate):
    grid_block = lax.all_to_all(iterate, "gc", split_axis=1, concat_axis=0, tiled=True)
    column_panel = lax.all_gather(grid_block, "gr", axis=0, tiled=True)
    rows_slice = column_panel
    gram_tile = lax.psum_scatter(
        lax.dot_general(
            rows_slice, grid_block, (((1,), (1,)), ((), ())), preferred_element_type=jnp.float32
        ).astype(jnp.bfloat16),
        "gc",
        scatter_dimension=0,
        tiled=True,
    )
    gram_rows = lax.all_gather(gram_tile, "gr", axis=1, tiled=True)
    rows_slice = gram_rows
    squared = lax.psum_scatter(
        lax.dot_general(
            rows_slice, gram_tile, (((0,), (0,)), ((), ())), preferred_element_type=jnp.float32
        ).astype(jnp.bfloat16),
        "gc",
        scatter_dimension=0,
        tiled=True,
    ).astype(jnp.float32)
    poly_tile = (CUBIC_COEF * gram_tile.astype(jnp.float32) + QUINTIC_COEF * squared).astype(
        jnp.bfloat16
    )
    rows_slice = column_panel
    applied = lax.dot_general(
        lax.all_gather(poly_tile, "gc", axis=0, tiled=True),
        rows_slice,
        (((0,), (0,)), ((), ())),
        preferred_element_type=jnp.float32,
    )
    update_scale = 0.2 * math.sqrt(max(M, N))
    result_block = ((LINEAR_COEF * grid_block.astype(jnp.float32) + applied) * update_scale).astype(
        jnp.bfloat16
    )
    return lax.all_to_all(result_block, "gc", split_axis=0, concat_axis=1, tiled=True)


def solution(mesh):
    in_specs = (P(("gr", "gc"), None),)
    out_specs = P(("gr", "gc"), None)
    return jax.shard_map(body, mesh=mesh, in_specs=in_specs, out_specs=out_specs, check_vma=False)
```

profile of v0, /device:TPU:1, one launch (start us, length us, event | category | flops | bytes accessed | tf_op | source)
XLA Modules:
  0.0 520.0 jit_solution(12225520010719391437)
XLA Ops:
  6.5 0.0 all-gather.4.cloned.1.call-start
  6.5 1.4 copy.10
  7.9 0.1 slice
  8.0 0.2 copy.7
  8.2 27.7 %all_to_all.38 = bf16[28,16,1152]{2,0,1:T(8,128)(2,1)S(1)} all-to-all(bf16[28,16,1152]{2,0,1:T(8,128)(2,1)S(1)} %copy.7), channel_id=1, replica_groups=mesh['gr'=8,'gc'=16] {'gc'}, dimensions={1} | all-to-all | bytes 2064384 | tf_op jit(solution)/shard_map/all_to_all | solution.py:18
  36.0 1.1 all_to_all.31
  37.0 0.0 all-gather.4.cloned.1.call-update
  37.1 0.0 reduce-scatter.3.cloned.1.call-start
  37.1 163.4 %all-gather.4.cloned.1.call-done = bf16[3584,1152]{1,0:T(8,128)(2,1)} async-done(((bf16[448,1152]{1,0:T(8,128)(2,1)}), bf16[3584,1152]{1,0:T(8,128)(2,1)}) %all-gather.4.cloned.1.call-update) | async-done | bytes 8257552 | tf_op jit(solution)/shard_map/all_gather | solution.py:19
  200.5 10.4 %convolution_convert_fusion.1 = bf16[3584,448]{1,0:T(8,128)(2,1)} fusion(bf16[3584,1152]{1,0:T(8,128)(2,1)} %all-gather.4.cloned.1.call-done, bf16[448,1152]{1,0:T(8,128)(2,1)} %all_to_all.31), kind=kOutput, calls=%fused_computation.1 | convolution fusion | flops 3700981760 | bytes 12500992 | tf_op jit(solution)/shard_map/dot_general | solution.py:22
  210.9 0.0 reduce-scatter.3.cloned.1.call-update
  210.9 0.0 all-gather.6.cloned.1.call-start
  210.9 81.5 %reduce-scatter.3.cloned.1.call-done = bf16[224,448]{1,0:T(8,128)(2,1)} async-done(((bf16[3584,448]{1,0:T(8,128)(2,1)}), bf16[224,448]{1,0:T(8,128)(2,1)}) %reduce-scatter.3.cloned.1.call-update) | async-done | bytes 200720 | tf_op jit(solution)/shard_map/reduce_scatter | solution.py:21
  292.4 1.8 copy.8
  294.2 0.0 all-gather.6.cloned.1.call-update
  294.2 0.0 reduce-scatter.5.cloned.1.call-start
  294.2 45.2 %all-gather.6.cloned.1.call-done = bf16[224,3584]{0,1:T(8,128)(2,1)} async-done(((bf16[224,448]{0,1:T(8,128)(2,1)}), bf16[224,3584]{0,1:T(8,128)(2,1)}) %all-gather.6.cloned.1.call-update) | async-done | bytes 1605648 | tf_op jit(solution)/shard_map/all_gather | solution.py:29
  339.4 4.4 convolution_convert_fusion
  343.8 0.0 copy-start.1
  343.8 0.0 copy-start
  343.8 0.0 reduce-scatter.5.cloned.1.call-update
  343.9 0.0 all-gather.8.cloned.1.call-start
  343.9 79.3 %reduce-scatter.5.cloned.1.call-done = bf16[224,448]{1,0:T(8,128)(2,1)} async-done(((bf16[3584,448]{1,0:T(8,128)(2,1)}), bf16[224,448]{1,0:T(8,128)(2,1)}) %reduce-scatter.5.cloned.1.call-update) | async-done | bytes 200720 | tf_op jit(solution)/shard_map/reduce_scatter | solution.py:31
  423.2 0.0 copy-done.1
  423.2 1.7 add_convert_fusion
  424.9 0.0 all-gather.8.cloned.1.call-update
  424.9 55.3 %all-gather.8.cloned.1.call-done = bf16[3584,448]{1,0:T(8,128)(2,1)} async-done(((bf16[224,448]{1,0:T(8,128)(2,1)}), bf16[3584,448]{1,0:T(8,128)(2,1)}) %all-gather.8.cloned.1.call-update) | async-done | bytes 3211280 | tf_op jit(solution)/shard_map/all_gather | solution.py:44
  480.2 0.0 copy-done
  480.2 8.8 %fusion.1 = bf16[448,1152]{1,0:T(8,128)(2,1)S(1)} fusion(bf16[3584,448]{1,0:T(8,128)(2,1)} %all-gather.8.cloned.1.call-done, bf16[3584,1152]{1,0:T(8,128)(2,1)} %all-gather.4.cloned.1.call-done, bf16[448,1152]{1,0:T(8,128)(2,1)S(1)} %copy-done), kind=kOutput, calls=%fused_computation.4 | convolution fusion | flops 3701956608 | bytes 13533184 | tf_op jit(solution)/shard_map/dot_general | solution.py:43
  489.1 0.3 all_to_all.32
  489.3 22.5 %all_to_all.39 = bf16[16,28,1152]{2,1,0:T(8,128)(2,1)S(1)} all-to-all(bf16[16,28,1152]{2,1,0:T(8,128)(2,1)S(1)} %all_to_all.32), channel_id=1, replica_groups=mesh['gr'=8,'gc'=16] {'gc'}, dimensions={0} | all-to-all | bytes 2064384 | tf_op jit(solution)/shard_map/all_to_all | solution.py:53
  511.9 0.3 copy.9
  512.2 0.1 pad
  512.3 1.2 copy.11
Async XLA Ops:
  6.5 194.0 %all-gather.4.cloned.1.call-start = ((), (), s32[]{:S(2)}) async-start(), calls=%async_computation.4 | async-start | bytes 9289728 | tf_op jit(solution)/shard_map/all_gather | solution.py:19
  37.1 255.3 %reduce-scatter.3.cloned.1.call-start = ((), (), s32[]{:S(2)}) async-start(), calls=%async_computation.5 | async-start | bytes 3899392 | tf_op jit(solution)/shard_map/reduce_scatter | solution.py:21
  210.9 128.5 %all-gather.6.cloned.1.call-start = ((), (), s32[]{:S(2)}) async-start(), calls=%async_computation.6 | async-start | bytes 2064384 | tf_op jit(solution)/shard_map/all_gather | solution.py:29
  294.2 129.0 %reduce-scatter.5.cloned.1.call-start = ((), (), s32[]{:S(2)}) async-start(), calls=%async_computation.7 | async-start | bytes 3899392 | tf_op jit(solution)/shard_map/reduce_scatter | solution.py:31
  343.8 79.4 %copy-start.1 = (bf16[224,448]{1,0:T(8,128)(2,1)S(1)}, bf16[224,448]{1,0:T(8,128)(2,1)}, u32[]{:S(2)}) copy-start(bf16[224,448]{1,0:T(8,128)(2,1)} %reduce-scatter.3.cloned.1.call-done) | copy-start | bytes 602116
  343.8 136.4 %copy-start = (bf16[448,1152]{1,0:T(8,128)(2,1)S(1)}, bf16[448,1152]{1,0:T(8,128)(2,1)}, u32[]{:S(2)}) copy-start(bf16[448,1152]{1,0:T(8,128)(2,1)} %all_to_all.31) | copy-start | bytes 3096580
  343.9 136.3 %all-gather.8.cloned.1.call-start = ((), (), s32[]{:S(2)}) async-start(), calls=%async_computation.8 | async-start | bytes 3899392 | tf_op jit(solution)/shard_map/all_gather | solution.py:44
Sparse Core Ops, SparseCore 0:
  37.2 163.2 all-gather.3
  211.0 81.3 reduce-scatter.2
  294.3 45.0 all-gather.5
  344.0 79.1 reduce-scatter.4
  425.5 54.7 all-gather.7
where the time goes:
time: 520 us
  waiting for transfers between devices  425 us (82%)
  blocking collectives  50.3 us (10%)
  matrix products  23.6 us (5%)
  between operations  13.2 us (3%)
  local copies, waits for them, and re-layouts  6.39 us (1%)
    all_gather x1, waiting for transfers between devices, body(): column_panel = lax.all_gather(grid_block, 'gr', axis=0, tiled=True)  163 us
    reduce_scatter x1, waiting for transfers between devices, body(): lax.psum_scatter(lax.dot_general(rows_slice, grid_block, (((1,), (1,)), (...  81.5 us
    reduce_scatter x1, waiting for transfers between devices, body(): lax.psum_scatter(lax.dot_general(rows_slice, gram_tile, (((0,), (0,)), ((...  79.3 us
    all_gather x1, waiting for transfers between devices, body(): lax.all_gather(poly_tile, 'gc', axis=0, tiled=True)  55.3 us
    all_gather x1, waiting for transfers between devices, body(): gram_rows = lax.all_gather(gram_tile, 'gr', axis=1, tiled=True)  45.2 us
    all_to_all x1, blocking collectives, body(): lax.all_to_all(iterate, 'gc', split_axis=1, concat_axis=0, tiled=True)  27.7 us
    all_to_all x1, blocking collectives, body(): lax.all_to_all(result_block, 'gc', split_axis=0, concat_axis=1, tiled=True)  22.5 us
  transfers between devices with their start and end apart: 5, of which 5 were waited for; matrix products, arithmetic and copies ran while one was open for 0% of the time, Pallas kernels for 0%

commit v1 on v0

v1 whole, which is shorter than its diff:
```python
import math

import jax
import jax.numpy as jnp
from jax import lax
from jax.sharding import Mesh
from jax.sharding import PartitionSpec as P

M = 3584
N = 18432
LINEAR_COEF = 3.4445
CUBIC_COEF = -4.775
QUINTIC_COEF = 2.0315
UPDATE_SCALE = 0.2 * math.sqrt(max(M, N))

AXES = ("y", "zl", "zh", "x", "c")
SIZES = (4, 2, 2, 4, 2)
PLANE = ("zh", "zl", "x")
BAND = M // 8
PANEL = N // 16


def dot(a, b, dims):
    return lax.dot_general(a, b, (dims, ((), ())), preferred_element_type=jnp.float32)


def body(iterate):
    tile = lax.all_to_all(iterate, PLANE, split_axis=1, concat_axis=0, tiled=True)
    panel = lax.all_gather(tile, ("y", "c"), axis=0).reshape(4, M // 4, PANEL)
    partial = jnp.stack(
        [dot(tile, panel[j], ((1,), (1,))).astype(jnp.bfloat16) for j in range(4)]
    )
    pieces = lax.all_to_all(
        partial.reshape(16, BAND // 4, M // 4), PLANE, split_axis=0, concat_axis=0, tiled=True
    )
    piece = jnp.sum(pieces.astype(jnp.float32), axis=0).astype(jnp.bfloat16)
    gathered = lax.all_gather(piece, PLANE + ("c",), axis=0).reshape(4, 4, 2, BAND // 4, M // 4)
    gram = lax.dynamic_index_in_dim(gathered, lax.axis_index("c"), axis=2, keepdims=False)
    gram = gram.reshape(4, BAND, M // 4)

    def gram_times(blocks):
        return sum(dot(gram[j], blocks[j], ((1,), (0,))) for j in range(4))

    wide_tile = tile.astype(jnp.float32)
    inner = (CUBIC_COEF * wide_tile + QUINTIC_COEF * gram_times(panel)).astype(jnp.bfloat16)
    inner_panel = lax.all_gather(inner, ("y", "c"), axis=0).reshape(4, M // 4, PANEL)
    result = ((LINEAR_COEF * wide_tile + gram_times(inner_panel)) * UPDATE_SCALE).astype(
        jnp.bfloat16
    )
    return lax.all_to_all(result, PLANE, split_axis=0, concat_axis=1, tiled=True)


def solution(mesh):
    physical = Mesh(mesh.devices.reshape(SIZES), AXES)
    return jax.shard_map(
        body, mesh=physical, in_specs=P(AXES, None), out_specs=P(AXES, None), check_vma=False
    )
```

time: 520 us -> 290 us (0.56)
  waiting for transfers between devices: 425 us -> 144 us
  blocking collectives: 50.3 us -> 96.4 us
  local copies, waits for them, and re-layouts: 6.39 us -> 12.8 us
    reduce_scatter x2 -> x0, waiting for transfers between devices: 161 us -> none  [the longest x1 81.5 us: body(): lax.psum_scatter(lax.dot_general(rows_slice, grid_block, (((1,), (1,)), (...]
    all_gather x3, waiting for transfers between devices: 264 us -> 144 us  [the longest x1 48.6 us: body(): panel = lax.all_gather(tile, ('y', 'c'), axis=0).reshape(4, M // 4, PANEL)]
    all_to_all x2 -> x3, blocking collectives: 50.3 us -> 96.4 us  [the longest x1 46.1 us: body(): lax.all_to_all(partial.reshape(16, BAND // 4, M // 4), PLANE, split_axis=...]
    slice x0 -> x2, local copies, waits for them, and re-layouts: none -> 5.98 us  [the longest x1 3.71 us: body(): panel[j]]
    dot_general x3 -> x12, matrix products: 23.6 us -> 21.1 us  [dot(): lax.dot_general(a, b, (dims, ((), ())), preferred_element_type=jnp.float32)]
  transfers between devices with their start and end apart: 5 -> 3, of which waited for: 5 -> 3; matrix products, arithmetic and copies ran while one was open for 0% -> 0% of each run, Pallas kernels for 0% -> 0%
where the time goes in v1:
time: 290 us
  waiting for transfers between devices  144 us (50%)
  blocking collectives  96.4 us (33%)
  matrix products  21.1 us (7%)
  between operations  13.4 us (5%)
  local copies, waits for them, and re-layouts  12.8 us (4%)
    all_gather x1, waiting for transfers between devices, body(): panel = lax.all_gather(tile, ('y', 'c'), axis=0).reshape(4, M // 4, PANEL)  48.6 us
    all_gather x1, waiting for transfers between devices, body(): lax.all_gather(inner, ('y', 'c'), axis=0).reshape(4, M // 4, PANEL)  48.1 us
    all_gather x1, waiting for transfers between devices, body(): lax.all_gather(piece, PLANE + ('c',), axis=0)  47.4 us
    all_to_all x1, blocking collectives, body(): lax.all_to_all(partial.reshape(16, BAND // 4, M // 4), PLANE, split_axis=...  46.1 us
    all_to_all x1, blocking collectives, body(): lax.all_to_all(iterate, PLANE, split_axis=1, concat_axis=0, tiled=True)  25.6 us
    all_to_all x1, blocking collectives, body(): lax.all_to_all(result, PLANE, split_axis=0, concat_axis=1, tiled=True)  24.6 us
    dot_general x12, matrix products, dot(): lax.dot_general(a, b, (dims, ((), ())), preferred_element_type=jnp.float32)  21.1 us
  transfers between devices with their start and end apart: 3, of which 3 were waited for; matrix products, arithmetic and copies ran while one was open for 0% of the time, Pallas kernels for 0%

profile of v1, /device:TPU:1, one launch (start us, length us, event | category | flops | bytes accessed | tf_op | source)
XLA Modules:
  0.0 289.8 jit_solution(9390119437172247143)
XLA Ops:
  6.5 0.0 all-gather.6.cloned.1.call-start
  6.5 1.4 copy.9
  7.9 0.1 slice.80
  8.0 0.2 copy.7
  8.2 25.6 %all_to_all.43 = bf16[28,16,1152]{2,0,1:T(8,128)(2,1)S(1)} all-to-all(bf16[28,16,1152]{2,0,1:T(8,128)(2,1)S(1)} %copy.7), channel_id=1, replica_groups=mesh['y'=4,'zl'=2,'zh'=2,'x'=4,'c'=2] {'zh','zl','x'}, dimensions={1} | all-to-all | bytes 2064384 | tf_op jit(solution)/shard_map/all_to_all | solution.py:28
  33.9 1.1 all_gather.18
  34.9 0.0 all-gather.6.cloned.1.call-update
  35.0 0.0 all-gather.8.cloned.1.call-start
  35.0 0.3 all_to_all.34
  35.3 0.0 copy-start.8
  35.3 48.6 %all-gather.6.cloned.1.call-done = bf16[8,448,1152]{2,1,0:T(8,128)(2,1)} async-done(((bf16[1,448,1152]{2,1,0:T(8,128)(2,1)}), bf16[8,448,1152]{2,1,0:T(8,128)(2,1)}) %all-gather.6.cloned.1.call-update) | async-done | bytes 8257552 | tf_op jit(solution)/shard_map/all_gather | solution.py:29
  83.9 3.7 %fusion.15 = (bf16[2,448,1152]{2,1,0:T(8,128)(2,1)S(1)}, bf16[2,448,1152]{2,1,0:T(8,128)(2,1)S(1)}, bf16[2,448,1152]{2,1,0:T(8,128)(2,1)S(1)}, bf16[2,448,1152]{2,1,0:T(8,128)(2,1)S(1)}) fusion(bf16[8,448,1152]{2,1,0:T(8,128)(2,1)} %all-gather.6.cloned.1.call-done), kind=kLoop, calls=%fused_computation.32 | loop fusion | bytes 16515072 | tf_op jit(solution)/shard_map/slice | solution.py:31
  87.6 0.0 copy-start
  87.6 0.0 copy-start.6
  87.7 0.0 copy-start.2
  87.7 0.0 copy-start.4
  87.7 1.3 fusion.14
  89.0 0.0 copy-done
  89.0 0.5 copy-done.6
  89.6 1.3 fusion.11
  90.9 0.0 copy-done.2
  90.9 1.3 fusion.13
  92.3 0.0 copy-done.8
  92.3 0.0 copy-done.4
  92.3 1.3 fusion.12
  93.6 0.5 pad_maximum_fusion
  94.2 46.1 %all_to_all.44 = bf16[16,112,896]{2,1,0:T(8,128)(2,1)S(1)} all-to-all(bf16[16,112,896]{2,1,0:T(8,128)(2,1)S(1)} %bitcast.46), channel_id=1, replica_groups=mesh['y'=4,'zl'=2,'zh'=2,'x'=4,'c'=2] {'zh','zl','x'}, dimensions={0} | all-to-all | bytes 6422528 | tf_op jit(solution)/shard_map/all_to_all | solution.py:33
  140.3 1.2 reduce_sum.12
  141.5 0.0 all-gather.8.cloned.1.call-update
  141.5 0.2 all-gather.10.cloned.1.call-start
  141.7 47.4 %all-gather.8.cloned.1.call-done = bf16[3584,896]{1,0:T(8,128)(2,1)} async-done(((bf16[112,896]{1,0:T(8,128)(2,1)}), bf16[3584,896]{1,0:T(8,128)(2,1)}) %all-gather.8.cloned.1.call-update) | async-done | bytes 6422544 | tf_op jit(solution)/shard_map/all_gather | solution.py:37
  189.1 0.0 copy-start.7
  189.1 2.3 constant_dynamic-slice_fusion.3
  191.3 0.0 copy-start.10
  191.4 0.0 copy-start.12
  191.4 0.3 copy-done.7
  191.6 0.0 copy-start.5
  191.6 1.3 fusion.16
  193.0 0.0 copy-done.10
  193.0 0.5 copy-done.5
  193.5 0.0 copy-start.3
  193.5 1.4 convolution_add_fusion.5
  194.9 0.0 copy-done.12
  194.9 0.2 copy-done.3
  195.1 0.0 copy-start.1
  195.1 1.4 convolution_add_fusion.4
  196.5 0.2 copy-done.1
  196.7 0.3 copy-done.9
  196.9 2.4 fusion.5
  199.3 0.0 all-gather.10.cloned.1.call-update
  199.3 48.1 %all-gather.10.cloned.1.call-done = bf16[3584,1152]{1,0:T(8,128)(2,1)} async-done(((bf16[448,1152]{1,0:T(8,128)(2,1)}), bf16[3584,1152]{1,0:T(8,128)(2,1)}) %all-gather.10.cloned.1.call-update) | async-done | bytes 8257552 | tf_op jit(solution)/shard_map/all_gather | solution.py:46
  247.4 3.3 %fusion.9 = f32[448,1152]{1,0:T(8,128)S(1)} fusion(bf16[448,896]{1,0:T(8,128)(2,1)} %bitcast.69, bf16[3584,1152]{1,0:T(8,128)(2,1)} %all-gather.10.cloned.1.call-done), kind=kOutput, calls=%fused_computation.18 | convolution fusion | flops 924844032 | bytes 4931584 | tf_op jit(solution)/shard_map/dot_general | solution.py:24
  250.7 0.0 copy-done.11
  250.7 0.0 slice-start.1
  250.8 3.1 %convolution_add_fusion.2 = f32[448,1152]{1,0:T(8,128)S(1)} fusion(f32[448,1152]{1,0:T(8,128)S(1)} %fusion.9, bf16[448,896]{1,0:T(8,128)(2,1)S(1)} %bitcast.67, bf16[3584,1152]{1,0:T(8,128)(2,1)} %all-gather.10.cloned.1.call-done), kind=kOutput, calls=%fused_computation.2 | convolution fusion | flops 925360128 | bytes 6995968 | tf_op jit(solution)/shard_map/dot_general | solution.py:24
  253.9 0.0 slice-done
  253.9 0.0 slice-done.1
  253.9 1.4 convolution_add_fusion.1
  255.3 1.4 fusion.4
  256.7 0.3 all_to_all.36
  257.0 24.6 %all_to_all.45 = bf16[16,28,1152]{2,1,0:T(8,128)(2,1)S(1)} all-to-all(bf16[16,28,1152]{2,1,0:T(8,128)(2,1)S(1)} %all_to_all.36), channel_id=1, replica_groups=mesh['y'=4,'zl'=2,'zh'=2,'x'=4,'c'=2] {'zh','zl','x'}, dimensions={0} | all-to-all | bytes 2064384 | tf_op jit(solution)/shard_map/all_to_all | solution.py:50
  281.6 0.3 copy.8
  281.9 0.1 pad.4
  282.0 1.2 copy.10
  (4 shorter events, 0.0 us)
Async XLA Ops:
  6.5 77.4 %all-gather.6.cloned.1.call-start = ((), (), s32[]{:S(2)}) async-start(), calls=%async_computation.3 | async-start | bytes 9289728 | tf_op jit(solution)/shard_map/all_gather | solution.py:29
  35.0 154.1 %all-gather.8.cloned.1.call-start = ((), (), s32[]{:S(2)}) async-start(), calls=%async_computation.4 | async-start | bytes 6623232 | tf_op jit(solution)/shard_map/all_gather | solution.py:37
  35.3 57.0 %copy-start.8 = (bf16[448,1152]{1,0:T(8,128)(2,1)}, bf16[448,1152]{1,0:T(8,128)(2,1)S(1)}, u32[]{:S(2)}) copy-start(bf16[448,1152]{1,0:T(8,128)(2,1)S(1)} %all_to_all.34) | copy-start | bytes 3096580
  87.6 1.4 copy-start
  87.6 1.9 copy-start.6
  87.7 3.3 %copy-start.2 = (bf16[2,448,1152]{2,1,0:T(8,128)(2,1)}, bf16[2,448,1152]{2,1,0:T(8,128)(2,1)S(1)}, u32[]{:S(2)}) copy-start(bf16[2,448,1152]{2,1,0:T(8,128)(2,1)S(1)} %get-tuple-element.7) | copy-start | bytes 6193156
  87.7 4.6 %copy-start.4 = (bf16[2,448,1152]{2,1,0:T(8,128)(2,1)}, bf16[2,448,1152]{2,1,0:T(8,128)(2,1)S(1)}, u32[]{:S(2)}) copy-start(bf16[2,448,1152]{2,1,0:T(8,128)(2,1)S(1)} %get-tuple-element.8) | copy-start | bytes 6193156
  141.5 105.9 %all-gather.10.cloned.1.call-start = ((), (), s32[]{:S(2)}) async-start(), calls=%async_computation.5 | async-start | bytes 9289728 | tf_op jit(solution)/shard_map/all_gather | solution.py:46
  189.1 2.5 copy-start.7
  191.3 1.6 copy-start.10
  191.4 3.6 %copy-start.12 = (bf16[1,4,1,112,896]{4,3,2,1,0:T(8,128)(2,1)}, bf16[1,4,1,112,896]{4,3,2,1,0:T(8,128)(2,1)S(1)}, u32[]{:S(2)}) copy-start(bf16[1,4,1,112,896]{4,3,2,1,0:T(8,128)(2,1)S(1)} %get-tuple-element.12) | copy-start | bytes 2408452
  191.6 1.9 copy-start.5
  193.5 1.6 copy-start.3
  195.1 1.6 copy-start.1
  195.1 1.8 copy-start.9
  247.4 3.3 %copy-start.11 = (bf16[1,4,1,112,896]{4,3,2,1,0:T(8,128)(2,1)S(1)}, bf16[1,4,1,112,896]{4,3,2,1,0:T(8,128)(2,1)}, u32[]{:S(2)}) copy-start(bf16[1,4,1,112,896]{4,3,2,1,0:T(8,128)(2,1)} %copy-done.10) | copy-start | bytes 2408452
  247.4 6.5 %slice-start = ((s8[8257536]{0:T(1024)(128)(4,1)}), s8[4194304]{0:T(1024)(128)(4,1)S(1)}, s32[]{:S(2)}) async-start(s8[8257536]{0:T(1024)(128)(4,1)} %bitcast.70), calls=%async_computation.6 | async-start | bytes 8388608
  250.7 3.1 %slice-start.1 = ((s8[8257536]{0:T(1024)(128)(4,1)}), s8[4063232]{0:T(1024)(128)(4,1)S(1)}, s32[]{:S(2)}) async-start(s8[8257536]{0:T(1024)(128)(4,1)} %bitcast.70), calls=%async_computation.7 | async-start | bytes 8126464
Sparse Core Ops, SparseCore 0:
  35.1 48.7 all-gather.5
  141.6 47.4 all-gather.7
  199.5 47.9 all-gather.9

commit v2 on v1

v2 whole, which is shorter than its diff:
```python
import math

import jax
import jax.numpy as jnp
import numpy as np
from jax import lax
from jax.sharding import Mesh
from jax.sharding import PartitionSpec as P

M = 3584
N = 18432
LINEAR_COEF = 3.4445
CUBIC_COEF = -4.775
QUINTIC_COEF = 2.0315
UPDATE_SCALE = 0.2 * math.sqrt(max(M, N))

AXES = ("y", "zl", "zh", "x", "c")
SIZES = (4, 2, 2, 4, 2)
PLANE = ("zh", "zl", "x")
BAND = M // 8
PANEL = N // 16
NEAR_STRIP = 88
FAR_STRIP = 32


def dot(a, b, dims):
    return lax.dot_general(a, b, (dims, ((), ())), preferred_element_type=jnp.float32)


def move(a, dy=0, dc=0):
    index = np.arange(math.prod(SIZES)).reshape(SIZES)
    target = np.roll(np.roll(index, -dy, axis=0), -dc, axis=4)
    pairs = [(int(s), int(t)) for s, t in zip(index.ravel(), target.ravel())]
    return lax.ppermute(a, AXES, pairs)


def trade(a):
    return lax.all_to_all(a, PLANE, split_axis=0, concat_axis=0, tiled=True)


def forward(below, above):
    half = BAND // 2
    return move(below[:half], dy=1), move(above[half:], dy=-1)


def with_other_core(total):
    from_other = move(total[BAND:].astype(jnp.bfloat16), dc=1)
    return total[:BAND] + from_other.astype(jnp.float32)


def plane_sum(partial, rows):
    partial = jnp.pad(partial, ((0, 16 * rows - partial.shape[0]), (0, 0)))
    terms = trade(partial.reshape(16, rows, M // 4))
    return jnp.sum(terms.astype(jnp.float32), axis=0).astype(jnp.bfloat16), terms


def body(iterate):
    tile = trade(iterate.reshape(M // 128, 16, PANEL).transpose(1, 0, 2)).reshape(BAND, PANEL)
    below, above = move(tile, dy=1), move(tile, dy=-1)
    band = jnp.concatenate([tile, move(tile, dc=1)])

    def columns(rows):
        return dot(rows, band, ((1,), (1,))).astype(jnp.bfloat16)

    part, below, above = lax.optimization_barrier((columns(tile), below, above))
    far_low, far_high = forward(below, above)
    partial = jnp.concatenate([part, columns(below), columns(above)])
    strip, terms = plane_sum(partial, NEAR_STRIP)
    strip, terms, far_low, far_high = lax.optimization_barrier((strip, terms, far_low, far_high))
    gram = lax.all_gather(strip, PLANE, axis=0, tiled=True)
    far = jnp.concatenate([far_low, far_high])
    strip, _ = plane_sum(columns(far), FAR_STRIP)
    gram_far = trade(jnp.broadcast_to(strip, (16,) + strip.shape)).reshape(-1, M // 4)
    panel = jnp.concatenate([tile, below, above])
    rows = [gram[j * BAND : (j + 1) * BAND] for j in range(3)] + [gram_far[:BAND]]

    wide_tile = tile.astype(jnp.float32)
    cubed = dot(rows[3], far, ((0,), (0,))) + dot(gram[: 3 * BAND], panel, ((0,), (0,)))
    inner = CUBIC_COEF * wide_tile + QUINTIC_COEF * with_other_core(cubed)
    inner = inner.astype(jnp.bfloat16)

    below, above = move(inner, dy=1), move(inner, dy=-1)
    total, below, above = lax.optimization_barrier(
        (dot(rows[0], inner, ((0,), (0,))), below, above)
    )
    far_low, far_high = forward(below, above)
    total = total + dot(rows[1], below, ((0,), (0,))) + dot(rows[2], above, ((0,), (0,)))
    total, far_low, far_high = lax.optimization_barrier((total, far_low, far_high))
    total = total + dot(rows[3], jnp.concatenate([far_low, far_high]), ((0,), (0,)))
    update = UPDATE_SCALE * (LINEAR_COEF * wide_tile + with_other_core(total))
    update = trade(update.astype(jnp.bfloat16).reshape(16, M // 128, PANEL))
    return update.transpose(1, 0, 2).reshape(M // 128, N)


def solution(mesh):
    physical = Mesh(mesh.devices.reshape(SIZES), AXES)
    return jax.shard_map(
        body, mesh=physical, in_specs=P(AXES, None), out_specs=P(AXES, None), check_vma=False
    )
```

time: 290 us -> 252 us (0.87)
  waiting for transfers between devices: 144 us -> 93.7 us
  starting transfers between devices: 0.27 us -> 20.4 us
  blocking collectives: 96.4 us -> 88 us
    all_gather x3 -> x1, waiting for transfers between devices: 144 us -> 7.91 us  [body(): gram = lax.all_gather(strip, PLANE, axis=0, tiled=True)]
    ppermute x0 -> x11, waiting for transfers between devices: none -> 54.3 us  [move(): return lax.ppermute(a, AXES, pairs)]
    all_to_all x0 -> x1, waiting for transfers between devices: none -> 31.4 us  [trade(): return lax.all_to_all(a, PLANE, split_axis=0, concat_axis=0, tiled=True)]
    ppermute x0 -> x11, starting transfers between devices: none -> 16.6 us  [move(): return lax.ppermute(a, AXES, pairs)]
    all_to_all x3 -> x4, blocking collectives: 96.4 us -> 88 us  [trade(): return lax.all_to_all(a, PLANE, split_axis=0, concat_axis=0, tiled=True)]
    all_to_all x0 -> x1, starting transfers between devices: none -> 3.73 us  [trade(): return lax.all_to_all(a, PLANE, split_axis=0, concat_axis=0, tiled=True)]
    slice x2 -> x7, local copies, waits for them, and re-layouts: 5.98 us -> 4.09 us  [the longest x4 3.81 us: forward(): return (move(below[:half], dy=1), move(above[half:], dy=-1))]
    dot_general x12 -> x10, matrix products: 21.1 us -> 20.1 us  [dot(): lax.dot_general(a, b, (dims, ((), ())), preferred_element_type=jnp.float32)]
  transfers between devices with their start and end apart: 3 -> 13, of which waited for: 3 -> 7; matrix products, arithmetic and copies ran while one was open for 0% -> 6% of each run, Pallas kernels for 0% -> 0%
where the time goes in v2:
time: 252 us; the launch traced here: 251 us
  waiting for transfers between devices  93.7 us (37%)
  blocking collectives  88 us (35%)
  starting transfers between devices  20.4 us (8%)
  matrix products  20.1 us (8%)
  between operations  13.7 us (5%)
  local copies, waits for them, and re-layouts  11.4 us (5%)
  other arithmetic  4.24 us (2%)
    all_to_all x4, blocking collectives, trade(): return lax.all_to_all(a, PLANE, split_axis=0, concat_axis=0, tiled=True)  88 us
    ppermute x11, waiting for transfers between devices, move(): return lax.ppermute(a, AXES, pairs)  54.3 us
    all_to_all x1, waiting for transfers between devices, trade(): return lax.all_to_all(a, PLANE, split_axis=0, concat_axis=0, tiled=True)  31.4 us
    dot_general x10, matrix products, dot(): lax.dot_general(a, b, (dims, ((), ())), preferred_element_type=jnp.float32)  20.1 us
    ppermute x11, starting transfers between devices, move(): return lax.ppermute(a, AXES, pairs)  16.6 us
    all_gather x1, waiting for transfers between devices, body(): gram = lax.all_gather(strip, PLANE, axis=0, tiled=True)  7.91 us
  transfers between devices with their start and end apart: 13, of which 7 were waited for; matrix products, arithmetic and copies ran while one was open for 6% of the time, Pallas kernels for 0%

profile of v2, /device:TPU:1, one launch (start us, length us, event | category | flops | bytes accessed | tf_op | source)
XLA Modules:
  0.0 251.5 jit_solution(6917239191775222320)
XLA Ops:
  6.5 1.4 copy.7
  7.9 0.1 slice.67
  8.0 0.2 copy.10
  8.2 25.6 %all_to_all.25 = bf16[16,28,1152]{2,1,0:T(8,128)(2,1)S(1)} all-to-all(bf16[16,28,1152]{2,1,0:T(8,128)(2,1)S(1)} %bitcast.31), channel_id=1, replica_groups=mesh['y'=4,'zl'=2,'zh'=2,'x'=4,'c'=2] {'zh','zl','x'}, dimensions={0} | all-to-all | bytes 2064384 | tf_op jit(solution)/shard_map/all_to_all | solution.py:38
  33.9 0.2 reshape.21
  34.1 2.2 collective-permute-start
  36.3 1.3 collective-permute-start.1
  37.6 1.4 collective-permute-start.2
  39.0 0.1 constant_dynamic-update-slice_fusion.1
  39.1 0.0 collective-permute-done
  39.1 0.1 constant_dynamic-update-slice_fusion
  39.3 1.3 fusion.18
  40.6 21.3 %collective-permute-done.1 = bf16[448,1152]{1,0:T(8,128)(2,1)S(1)} collective-permute-done((bf16[448,1152]{1,0:T(8,128)(2,1)S(1)}, bf16[448,1152]{1,0:T(8,128)(2,1)S(1)}, u32[]{:S(2)}, u32[]{:S(2)}) %collective-permute-start.1) | collective-permute-done | bytes 1032224 | tf_op jit(solution)/shard_map/ppermute | solution.py:34
  62.0 1.0 copy-done.1
  63.0 1.3 convolution_convert_fusion.2
  64.4 1.3 convolution_convert_fusion.1
  65.7 1.7 fusion.10
  67.4 3.7 %all-to-all-start.1 = ((bf16[16,88,896]{2,1,0:T(8,128)(2,1)}), bf16[16,88,896]{2,1,0:T(8,128)(2,1)S(1)}, u32[]{:S(2)}, u32[]{:S(2)}) async-start(bf16[16,88,896]{2,1,0:T(8,128)(2,1)} %bitcast.29), calls=%async_computation.1 | async-start | bytes 5046272 | tf_op jit(solution)/shard_map/all_to_all | solution.py:38
  71.1 0.0 all-gather.2.cloned.1.call-start
  71.2 1.9 slice.44
  73.1 1.8 slice.45
  74.9 0.0 collective-permute-start.3
  74.9 2.7 %collective-permute-start.4 = (bf16[224,1152]{1,0:T(8,128)(2,1)}, bf16[224,1152]{1,0:T(8,128)(2,1)}, u32[]{:S(2)}, u32[]{:S(2)}) collective-permute-start(bf16[224,1152]{1,0:T(8,128)(2,1)} %slice.45), channel_id=1, source_target_pairs={{0,96},{1,97},{2,98},{3,99},{4,100},{5,101},{6,102},{7,103},{8,104... | collective-permute-start | bytes 1548296 | tf_op jit(solution)/shard_map/ppermute | solution.py:34
  77.6 31.4 %all-to-all-done.1 = bf16[16,88,896]{2,1,0:T(8,128)(2,1)S(1)} async-done(((bf16[16,88,896]{2,1,0:T(8,128)(2,1)}), bf16[16,88,896]{2,1,0:T(8,128)(2,1)S(1)}, u32[]{:S(2)}, u32[]{:S(2)}) %all-to-all-start.1) | async-done | bytes 2523168 | tf_op jit(solution)/shard_map/all_to_all | solution.py:38
  109.0 1.1 reduce_sum.24
  110.1 0.0 all-gather.2.cloned.1.call-update
  110.1 1.1 constant_dynamic-update-slice_fusion.3
  111.2 1.1 constant_dynamic-update-slice_fusion.2
  112.3 2.9 %convolution_convert_fusion = bf16[448,896]{1,0:T(8,128)(2,1)S(1)} fusion(bf16[448,1152]{1,0:T(8,128)(2,1)S(1)} %constant_dynamic-update-slice_fusion.2, bf16[896,1152]{1,0:T(8,128)(2,1)} %copy-done), kind=kOutput, calls=%fused_computation.27 | convolution fusion | flops 925245440 | bytes 3899392 | tf_op jit(solution)/shard_map/dot_general | solution.py:27
  115.2 0.1 pad.9
  115.3 19.9 %all_to_all.26 = bf16[16,32,896]{2,1,0:T(8,128)(2,1)S(1)} all-to-all(bf16[16,32,896]{2,1,0:T(8,128)(2,1)S(1)} %bitcast.34), channel_id=1, replica_groups=mesh['y'=4,'zl'=2,'zh'=2,'x'=4,'c'=2] {'zh','zl','x'}, dimensions={0} | all-to-all | bytes 1835008 | tf_op jit(solution)/shard_map/all_to_all | solution.py:38
  135.2 0.1 reduce_sum.25
  135.3 0.1 broadcast_in_dim.3
  135.4 20.4 %all_to_all.27 = bf16[16,32,896]{2,1,0:T(8,128)(2,1)S(1)} all-to-all(bf16[16,32,896]{2,1,0:T(8,128)(2,1)S(1)} %broadcast_in_dim.3), channel_id=1, replica_groups=mesh['y'=4,'zl'=2,'zh'=2,'x'=4,'c'=2] {'zh','zl','x'}, dimensions={0} | all-to-all | bytes 1835008 | tf_op jit(solution)/shard_map/all_to_all | solution.py:38
  155.8 0.1 slice.59
  155.9 7.9 %all-gather.2.cloned.1.call-done = bf16[1408,896]{1,0:T(8,128)(2,1)} async-done(((bf16[88,896]{1,0:T(8,128)(2,1)}), bf16[1408,896]{1,0:T(8,128)(2,1)}) %all-gather.2.cloned.1.call-update) | async-done | bytes 2523152 | tf_op jit(solution)/shard_map/all_gather | solution.py:70
  163.8 6.0 %fusion.3 = f32[896,1152]{1,0:T(8,128)S(1)} fusion(bf16[448,1152]{1,0:T(8,128)(2,1)} %copy-done.2, bf16[448,1152]{1,0:T(8,128)(2,1)} %copy-done.1, bf16[448,1152]{1,0:T(8,128)(2,1)S(1)} %reshape.21, bf16[1408,896]{1,0:T(8,128)(2,1)} %all-gather.2.cloned.1.call-done), kind=kOutput, calls=%fused_computation.6 | convolution fusion | flops 2783821824 | bytes 9633792 | tf_op jit(solution)/shard_map/dot_general | solution.py:27
  169.8 1.4 convolution_add_fusion
  171.2 0.1 slice.89
  171.3 1.1 collective-permute-start.5
  172.4 2.3 collective-permute-done.5
  174.7 0.5 fusion.16
  175.1 0.1 collective-permute-start.6
  175.2 2.7 %collective-permute-start.7 = (bf16[448,1152]{1,0:T(8,128)(2,1)S(1)}, bf16[448,1152]{1,0:T(8,128)(2,1)S(1)}, u32[]{:S(2)}, u32[]{:S(2)}) collective-permute-start(bf16[448,1152]{1,0:T(8,128)(2,1)S(1)} %fusion.16), channel_id=1, source_target_pairs={{0,96},{1,97},{2,98},{3,99},{4,100},{5,101},{6,102},{7,103},{8,104... | collective-permute-start | bytes 3096584 | tf_op jit(solution)/shard_map/ppermute | solution.py:34
  177.9 1.4 fusion.29
  179.3 21.1 %collective-permute-done.6 = bf16[448,1152]{1,0:T(8,128)(2,1)S(1)} collective-permute-done((bf16[448,1152]{1,0:T(8,128)(2,1)S(1)}, bf16[448,1152]{1,0:T(8,128)(2,1)S(1)}, u32[]{:S(2)}, u32[]{:S(2)}) %collective-permute-start.6) | collective-permute-done | bytes 1032224 | tf_op jit(solution)/shard_map/ppermute | solution.py:34
  200.4 0.0 collective-permute-done.7
  200.5 0.1 collective-permute-start.8
  200.6 2.9 %collective-permute-start.9 = (bf16[224,1152]{1,0:T(8,128)(2,1)S(1)}, bf16[224,1152]{1,0:T(8,128)(2,1)S(1)}, u32[]{:S(2)}, u32[]{:S(2)}) collective-permute-start(bf16[224,1152]{1,0:T(8,128)(2,1)S(1)} %slice.55), channel_id=1, source_target_pairs={{0,96},{1,97},{2,98},{3,99},{4,100},{5,101},{6,102},{7,103},{8,104... | collective-permute-start | bytes 1548296 | tf_op jit(solution)/shard_map/ppermute | solution.py:34
  203.6 1.4 fusion.27
  205.0 1.6 add_add_fusion
  206.5 7.3 %collective-permute-done.8 = bf16[224,1152]{1,0:T(8,128)(2,1)S(1)} collective-permute-done((bf16[224,1152]{1,0:T(8,128)(2,1)S(1)}, bf16[224,1152]{1,0:T(8,128)(2,1)S(1)}, u32[]{:S(2)}, u32[]{:S(2)}) %collective-permute-start.8) | collective-permute-done | bytes 516128 | tf_op jit(solution)/shard_map/ppermute | solution.py:34
  213.8 0.0 collective-permute-done.9
  213.8 1.4 fusion.19
  215.2 0.4 add.33
  215.6 0.1 slice.88
  215.7 2.2 collective-permute-start.10
  217.9 2.3 collective-permute-done.10
  220.2 0.5 fusion.14
  220.7 0.3 reshape.24
  220.9 22.0 %all_to_all.28 = bf16[16,28,1152]{2,1,0:T(8,128)(2,1)S(1)} all-to-all(bf16[16,28,1152]{2,1,0:T(8,128)(2,1)S(1)} %reshape.24), channel_id=1, replica_groups=mesh['y'=4,'zl'=2,'zh'=2,'x'=4,'c'=2] {'zh','zl','x'}, dimensions={0} | all-to-all | bytes 2064384 | tf_op jit(solution)/shard_map/all_to_all | solution.py:38
  243.0 0.3 copy.6
  243.3 0.1 pad.21
  243.4 1.2 copy.8
  (12 shorter events, 0.1 us)
Async XLA Ops:
  34.1 5.0 %collective-permute-start = (bf16[448,1152]{1,0:T(8,128)(2,1)S(1)}, bf16[448,1152]{1,0:T(8,128)(2,1)S(1)}, u32[]{:S(2)}, u32[]{:S(2)}) collective-permute-start(bf16[448,1152]{1,0:T(8,128)(2,1)S(1)} %reshape.21), channel_id=1, source_target_pairs={{0,1},{1,0},{2,3},{3,2},{4,5},{5,4},{6,7},{7,6},{8,9},{9,8},{10,11... | collective-permute-start | bytes 3096584 | tf_op jit(solution)/shard_map/ppermute | solution.py:34
  36.3 25.7 %collective-permute-start.1 = (bf16[448,1152]{1,0:T(8,128)(2,1)S(1)}, bf16[448,1152]{1,0:T(8,128)(2,1)S(1)}, u32[]{:S(2)}, u32[]{:S(2)}) collective-permute-start(bf16[448,1152]{1,0:T(8,128)(2,1)S(1)} %reshape.21), channel_id=1, source_target_pairs={{0,32},{1,33},{2,34},{3,35},{4,36},{5,37},{6,38},{7,39},{8,40},{9,... | collective-permute-start | bytes 3096584 | tf_op jit(solution)/shard_map/ppermute | solution.py:34
  37.6 24.4 %collective-permute-start.2 = (bf16[448,1152]{1,0:T(8,128)(2,1)S(1)}, bf16[448,1152]{1,0:T(8,128)(2,1)S(1)}, u32[]{:S(2)}, u32[]{:S(2)}) collective-permute-start(bf16[448,1152]{1,0:T(8,128)(2,1)S(1)} %reshape.21), channel_id=1, source_target_pairs={{0,96},{1,97},{2,98},{3,99},{4,100},{5,101},{6,102},{7,103},{8,104... | collective-permute-start | bytes 3096584 | tf_op jit(solution)/shard_map/ppermute | solution.py:34
  39.3 25.1 %copy-start = (bf16[896,1152]{1,0:T(8,128)(2,1)}, bf16[896,1152]{1,0:T(8,128)(2,1)S(1)}, u32[]{:S(2)}) copy-start(bf16[896,1152]{1,0:T(8,128)(2,1)S(1)} %constant_dynamic-update-slice_fusion) | copy-start | bytes 6193156
  62.0 1.0 copy-start.1
  63.0 1.4 copy-start.2
  67.4 41.6 %all-to-all-start.1 = ((bf16[16,88,896]{2,1,0:T(8,128)(2,1)}), bf16[16,88,896]{2,1,0:T(8,128)(2,1)S(1)}, u32[]{:S(2)}, u32[]{:S(2)}) async-start(bf16[16,88,896]{2,1,0:T(8,128)(2,1)} %bitcast.29), calls=%async_computation.1 | async-start | bytes 5046272 | tf_op jit(solution)/shard_map/all_to_all | solution.py:38
  71.1 92.7 %all-gather.2.cloned.1.call-start = ((), (), s32[]{:S(2)}) async-start(), calls=%async_computation.5 | async-start | bytes 2680832 | tf_op jit(solution)/shard_map/all_gather | solution.py:70
  74.9 35.2 %collective-permute-start.3 = (bf16[224,1152]{1,0:T(8,128)(2,1)}, bf16[224,1152]{1,0:T(8,128)(2,1)}, u32[]{:S(2)}, u32[]{:S(2)}) collective-permute-start(bf16[224,1152]{1,0:T(8,128)(2,1)} %slice.44), channel_id=1, source_target_pairs={{0,32},{1,33},{2,34},{3,35},{4,36},{5,37},{6,38},{7,39},{8,40},{9,... | collective-permute-start | bytes 1548296 | tf_op jit(solution)/shard_map/ppermute | solution.py:34
  74.9 35.2 %collective-permute-start.4 = (bf16[224,1152]{1,0:T(8,128)(2,1)}, bf16[224,1152]{1,0:T(8,128)(2,1)}, u32[]{:S(2)}, u32[]{:S(2)}) collective-permute-start(bf16[224,1152]{1,0:T(8,128)(2,1)} %slice.45), channel_id=1, source_target_pairs={{0,96},{1,97},{2,98},{3,99},{4,100},{5,101},{6,102},{7,103},{8,104... | collective-permute-start | bytes 1548296 | tf_op jit(solution)/shard_map/ppermute | solution.py:34
  171.3 6.6 %copy-start.3 = (bf16[1408,896]{1,0:T(8,128)(2,1)S(1)}, bf16[1408,896]{1,0:T(8,128)(2,1)}, u32[]{:S(2)}) copy-start(bf16[1408,896]{1,0:T(8,128)(2,1)} %all-gather.2.cloned.1.call-done) | copy-start | bytes 7569412
  171.3 3.3 %collective-permute-start.5 = (bf16[448,1152]{1,0:T(8,128)(2,1)S(1)}, bf16[448,1152]{1,0:T(8,128)(2,1)S(1)}, u32[]{:S(2)}, u32[]{:S(2)}) collective-permute-start(bf16[448,1152]{1,0:T(8,128)(2,1)S(1)} %slice.89), channel_id=1, source_target_pairs={{0,1},{1,0},{2,3},{3,2},{4,5},{5,4},{6,7},{7,6},{8,9},{9,8},{10,11... | collective-permute-start | bytes 3096584 | tf_op jit(solution)/shard_map/ppermute | solution.py:34
  175.1 25.3 %collective-permute-start.6 = (bf16[448,1152]{1,0:T(8,128)(2,1)S(1)}, bf16[448,1152]{1,0:T(8,128)(2,1)S(1)}, u32[]{:S(2)}, u32[]{:S(2)}) collective-permute-start(bf16[448,1152]{1,0:T(8,128)(2,1)S(1)} %fusion.16), channel_id=1, source_target_pairs={{0,32},{1,33},{2,34},{3,35},{4,36},{5,37},{6,38},{7,39},{8,40},{9,... | collective-permute-start | bytes 3096584 | tf_op jit(solution)/shard_map/ppermute | solution.py:34
  175.2 25.2 %collective-permute-start.7 = (bf16[448,1152]{1,0:T(8,128)(2,1)S(1)}, bf16[448,1152]{1,0:T(8,128)(2,1)S(1)}, u32[]{:S(2)}, u32[]{:S(2)}) collective-permute-start(bf16[448,1152]{1,0:T(8,128)(2,1)S(1)} %fusion.16), channel_id=1, source_target_pairs={{0,96},{1,97},{2,98},{3,99},{4,100},{5,101},{6,102},{7,103},{8,104... | collective-permute-start | bytes 3096584 | tf_op jit(solution)/shard_map/ppermute | solution.py:34
  200.5 13.3 %collective-permute-start.8 = (bf16[224,1152]{1,0:T(8,128)(2,1)S(1)}, bf16[224,1152]{1,0:T(8,128)(2,1)S(1)}, u32[]{:S(2)}, u32[]{:S(2)}) collective-permute-start(bf16[224,1152]{1,0:T(8,128)(2,1)S(1)} %slice.54), channel_id=1, source_target_pairs={{0,32},{1,33},{2,34},{3,35},{4,36},{5,37},{6,38},{7,39},{8,40},{9,... | collective-permute-start | bytes 1548296 | tf_op jit(solution)/shard_map/ppermute | solution.py:34
  200.6 13.2 %collective-permute-start.9 = (bf16[224,1152]{1,0:T(8,128)(2,1)S(1)}, bf16[224,1152]{1,0:T(8,128)(2,1)S(1)}, u32[]{:S(2)}, u32[]{:S(2)}) collective-permute-start(bf16[224,1152]{1,0:T(8,128)(2,1)S(1)} %slice.55), channel_id=1, source_target_pairs={{0,96},{1,97},{2,98},{3,99},{4,100},{5,101},{6,102},{7,103},{8,104... | collective-permute-start | bytes 1548296 | tf_op jit(solution)/shard_map/ppermute | solution.py:34
  215.7 4.5 %collective-permute-start.10 = (bf16[448,1152]{1,0:T(8,128)(2,1)S(1)}, bf16[448,1152]{1,0:T(8,128)(2,1)S(1)}, u32[]{:S(2)}, u32[]{:S(2)}) collective-permute-start(bf16[448,1152]{1,0:T(8,128)(2,1)S(1)} %slice.88), channel_id=1, source_target_pairs={{0,1},{1,0},{2,3},{3,2},{4,5},{5,4},{6,7},{7,6},{8,9},{9,8},{10,11... | collective-permute-start | bytes 3096584 | tf_op jit(solution)/shard_map/ppermute | solution.py:34
Sparse Core Ops, SparseCore 0:
  110.2 53.5 all-gather.1

commit v3 on v2

--- a/solution.py
+++ b/solution.py
@@ -19,7 +19,8 @@
 PLANE = ("zh", "zl", "x")
 BAND = M // 8
 PANEL = N // 16
-NEAR_STRIP = 88
+OWN_STRIP = 32
+NEAR_STRIP = 56
 FAR_STRIP = 32
 
 
@@ -48,10 +49,19 @@
     return total[:BAND] + from_other.astype(jnp.float32)
 
 
-def plane_sum(partial, rows):
+def terms_of_strips(partial, rows):
     partial = jnp.pad(partial, ((0, 16 * rows - partial.shape[0]), (0, 0)))
-    terms = trade(partial.reshape(16, rows, M // 4))
-    return jnp.sum(terms.astype(jnp.float32), axis=0).astype(jnp.bfloat16), terms
+    return trade(partial.reshape(16, rows, M // 4))
+
+
+def strip_of(terms):
+    return jnp.sum(terms.astype(jnp.float32), axis=0).astype(jnp.bfloat16)
+
+
+def in_strips(own, below, above):
+    own = jnp.pad(own, ((0, 16 * OWN_STRIP - BAND), (0, 0))).reshape(16, OWN_STRIP, PANEL)
+    near = jnp.concatenate([below, above]).reshape(16, NEAR_STRIP, PANEL)
+    return jnp.concatenate([own, near], axis=1).reshape(-1, PANEL)
 
 
 def body(iterate):
@@ -62,31 +72,30 @@
     def columns(rows):
         return dot(rows, band, ((1,), (1,))).astype(jnp.bfloat16)
 
-    part, below, above = lax.optimization_barrier((columns(tile), below, above))
+    own_terms = terms_of_strips(columns(tile), OWN_STRIP)
+    own_terms, below, above = lax.optimization_barrier((own_terms, below, above))
     far_low, far_high = forward(below, above)
-    partial = jnp.concatenate([part, columns(below), columns(above)])
-    strip, terms = plane_sum(partial, NEAR_STRIP)
-    strip, terms, far_low, far_high = lax.optimization_barrier((strip, terms, far_low, far_high))
+    near = jnp.concatenate([columns(below), columns(above)])
+    near_terms = terms_of_strips(near, NEAR_STRIP)
+    near_terms, far_low, far_high = lax.optimization_barrier((near_terms, far_low, far_high))
+    strip = jnp.concatenate([strip_of(own_terms), strip_of(near_terms)])
     gram = lax.all_gather(strip, PLANE, axis=0, tiled=True)
     far = jnp.concatenate([far_low, far_high])
-    strip, _ = plane_sum(columns(far), FAR_STRIP)
-    gram_far = trade(jnp.broadcast_to(strip, (16,) + strip.shape)).reshape(-1, M // 4)
-    panel = jnp.concatenate([tile, below, above])
-    rows = [gram[j * BAND : (j + 1) * BAND] for j in range(3)] + [gram_far[:BAND]]
+    strip = strip_of(terms_of_strips(columns(far), FAR_STRIP))
+    gram_far = trade(jnp.broadcast_to(strip, (16,) + strip.shape)).reshape(-1, M // 4)[:BAND]
+    panel = in_strips(tile, below, above)
 
     wide_tile = tile.astype(jnp.float32)
-    cubed = dot(rows[3], far, ((0,), (0,))) + dot(gram[: 3 * BAND], panel, ((0,), (0,)))
+    cubed, gram, panel = lax.optimization_barrier((dot(gram_far, far, ((0,), (0,))), gram, panel))
+    cubed = cubed + dot(gram, panel, ((0,), (0,)))
     inner = CUBIC_COEF * wide_tile + QUINTIC_COEF * with_other_core(cubed)
     inner = inner.astype(jnp.bfloat16)
 
     below, above = move(inner, dy=1), move(inner, dy=-1)
-    total, below, above = lax.optimization_barrier(
-        (dot(rows[0], inner, ((0,), (0,))), below, above)
-    )
     far_low, far_high = forward(below, above)
-    total = total + dot(rows[1], below, ((0,), (0,))) + dot(rows[2], above, ((0,), (0,)))
+    total = dot(gram, in_strips(inner, below, above), ((0,), (0,)))
     total, far_low, far_high = lax.optimization_barrier((total, far_low, far_high))
-    total = total + dot(rows[3], jnp.concatenate([far_low, far_high]), ((0,), (0,)))
+    total = total + dot(gram_far, jnp.concatenate([far_low, far_high]), ((0,), (0,)))
     update = UPDATE_SCALE * (LINEAR_COEF * wide_tile + with_other_core(total))
     update = trade(update.astype(jnp.bfloat16).reshape(16, M // 128, PANEL))
     return update.transpose(1, 0, 2).reshape(M // 128, N)

time: 252 us -> 246 us (0.976)
  blocking collectives: 88 us -> 69.4 us
  waiting for transfers between devices: 93.7 us -> 87.5 us
  starting transfers between devices: 20.4 us -> 26.2 us
  other arithmetic: 4.24 us -> 9.85 us
  matrix products: 20.1 us -> 24.9 us
  local copies, waits for them, and re-layouts: 11.4 us -> 14 us
    all_to_all x4 -> x3, blocking collectives: 88 us -> 69.4 us  [trade(): return lax.all_to_all(a, PLANE, split_axis=0, concat_axis=0, tiled=True)]
    all_to_all x1 -> x3, waiting for transfers between devices: 31.4 us -> 19.5 us  [trade(): return lax.all_to_all(a, PLANE, split_axis=0, concat_axis=0, tiled=True)]
    ppermute x11, waiting for transfers between devices: 54.3 us -> 65.3 us  [move(): return lax.ppermute(a, AXES, pairs)]
    all_to_all x1 -> x3, starting transfers between devices: 3.73 us -> 11.3 us  [trade(): return lax.all_to_all(a, PLANE, split_axis=0, concat_axis=0, tiled=True)]
    all_gather x1, waiting for transfers between devices: 7.91 us -> 2.72 us  [body(): gram = lax.all_gather(strip, PLANE, axis=0, tiled=True)]
    concatenate x1 -> x6, other arithmetic: 1.68 us -> 6.74 us  [the longest x2 2.21 us: in_strips(): return jnp.concatenate([own, near], axis=1).reshape(-1, PANEL)]
    dot_general x10 -> x8, matrix products: 20.1 us -> 24.9 us  [dot(): lax.dot_general(a, b, (dims, ((), ())), preferred_element_type=jnp.float32)]
    unnamed x13 -> x19, local copies, waits for them, and re-layouts: 4.89 us -> 5.34 us
  transfers between devices with their start and end apart: 13 -> 15, of which waited for: 7 -> 12; matrix products, arithmetic and copies ran while one was open for 6% -> 10% of each run, Pallas kernels for 0% -> 0%
where the time goes in v3:
time: 246 us
  waiting for transfers between devices  87.5 us (36%)
  blocking collectives  69.4 us (28%)
  starting transfers between devices  26.2 us (11%)
  matrix products  24.9 us (10%)
  local copies, waits for them, and re-layouts  14 us (6%)
  between operations  13.7 us (6%)
  other arithmetic  9.85 us (4%)
    all_to_all x3, blocking collectives, trade(): return lax.all_to_all(a, PLANE, split_axis=0, concat_axis=0, tiled=True)  69.4 us
    ppermute x11, waiting for transfers between devices, move(): return lax.ppermute(a, AXES, pairs)  65.3 us
    dot_general x8, matrix products, dot(): lax.dot_general(a, b, (dims, ((), ())), preferred_element_type=jnp.float32)  24.9 us
    all_to_all x3, waiting for transfers between devices, trade(): return lax.all_to_all(a, PLANE, split_axis=0, concat_axis=0, tiled=True)  19.5 us
    ppermute x11, starting transfers between devices, move(): return lax.ppermute(a, AXES, pairs)  14.8 us
    all_to_all x3, starting transfers between devices, trade(): return lax.all_to_all(a, PLANE, split_axis=0, concat_axis=0, tiled=True)  11.3 us
    unnamed x19, local copies, waits for them, and re-layouts  5.34 us
  transfers between devices with their start and end apart: 15, of which 12 were waited for; matrix products, arithmetic and copies ran while one was open for 10% of the time, Pallas kernels for 0%

profile of v3, /device:TPU:1, one launch (start us, length us, event | category | flops | bytes accessed | tf_op | source)
XLA Modules:
  0.0 245.6 jit_solution(9633769555128213884)
XLA Ops:
  6.5 1.4 copy.7
  8.0 0.2 copy.10
  8.2 25.6 %all_to_all.30 = bf16[16,28,1152]{2,1,0:T(8,128)(2,1)S(1)} all-to-all(bf16[16,28,1152]{2,1,0:T(8,128)(2,1)S(1)} %bitcast.44), channel_id=1, replica_groups=mesh['y'=4,'zl'=2,'zh'=2,'x'=4,'c'=2] {'zh','zl','x'}, dimensions={0} | all-to-all | bytes 2064384 | tf_op jit(solution)/shard_map/all_to_all | solution.py:39
  33.9 0.2 reshape.42
  34.1 2.2 collective-permute-start
  36.3 2.7 %collective-permute-start.2 = (bf16[448,1152]{1,0:T(8,128)(2,1)S(1)}, bf16[448,1152]{1,0:T(8,128)(2,1)S(1)}, u32[]{:S(2)}, u32[]{:S(2)}) collective-permute-start(bf16[448,1152]{1,0:T(8,128)(2,1)S(1)} %reshape.42), channel_id=1, source_target_pairs={{0,96},{1,97},{2,98},{3,99},{4,100},{5,101},{6,102},{7,103},{8,104... | collective-permute-start | bytes 3096584 | tf_op jit(solution)/shard_map/ppermute | solution.py:35
  39.1 0.1 constant_dynamic-update-slice_fusion
  39.3 1.3 fusion.6
  40.7 1.0 pad.14
  41.7 3.6 %all-to-all-start.1 = ((bf16[16,32,896]{2,1,0:T(8,128)(2,1)}), bf16[16,32,896]{2,1,0:T(8,128)(2,1)S(1)}, u32[]{:S(2)}, u32[]{:S(2)}) async-start(bf16[16,32,896]{2,1,0:T(8,128)(2,1)} %bitcast.2), calls=%async_computation.1 | async-start | bytes 1835008 | tf_op jit(solution)/shard_map/all_to_all | solution.py:39
  45.3 15.9 %collective-permute-done.2 = bf16[448,1152]{1,0:T(8,128)(2,1)S(1)} collective-permute-done((bf16[448,1152]{1,0:T(8,128)(2,1)S(1)}, bf16[448,1152]{1,0:T(8,128)(2,1)S(1)}, u32[]{:S(2)}, u32[]{:S(2)}) %collective-permute-start.2) | collective-permute-done | bytes 1032224 | tf_op jit(solution)/shard_map/ppermute | solution.py:35
  61.2 3.2 %collective-permute-done.1 = bf16[448,1152]{1,0:T(8,128)(2,1)} collective-permute-done((bf16[448,1152]{1,0:T(8,128)(2,1)S(1)}, bf16[448,1152]{1,0:T(8,128)(2,1)}, u32[]{:S(2)}, u32[]{:S(2)}) %collective-permute-start.1) | collective-permute-done | bytes 1032224 | tf_op jit(solution)/shard_map/ppermute | solution.py:35
  64.4 3.4 %convolution_convert_fusion.2 = bf16[448,896]{1,0:T(8,128)(2,1)S(1)} fusion(bf16[448,1152]{1,0:T(8,128)(2,1)} %collective-permute-done.1, bf16[896,1152]{1,0:T(8,128)(2,1)} %copy-done.3), kind=kOutput, calls=%fused_computation.20 | convolution fusion | flops 925245440 | bytes 3899392 | tf_op jit(solution)/shard_map/dot_general | solution.py:28
  67.8 1.3 convolution_convert_fusion.1
  69.1 1.3 pad_maximum_fusion.4
  70.4 3.7 %all-to-all-start.2 = ((bf16[16,56,896]{2,1,0:T(8,128)(2,1)}), bf16[16,56,896]{2,1,0:T(8,128)(2,1)S(1)}, u32[]{:S(2)}, u32[]{:S(2)}) async-start(bf16[16,56,896]{2,1,0:T(8,128)(2,1)} %bitcast.40), calls=%async_computation.2 | async-start | bytes 3211264 | tf_op jit(solution)/shard_map/all_to_all | solution.py:39
  74.2 1.9 slice.32
  76.1 1.9 slice.33
  78.0 0.5 collective-permute-start.4
  78.5 1.0 collective-permute-start.3
  79.4 0.7 reduce_sum.37
  80.2 10.2 %collective-permute-done.4 = bf16[224,1152]{1,0:T(8,128)(2,1)} collective-permute-done((bf16[224,1152]{1,0:T(8,128)(2,1)}, bf16[224,1152]{1,0:T(8,128)(2,1)}, u32[]{:S(2)}, u32[]{:S(2)}) %collective-permute-start.4) | collective-permute-done | bytes 516128 | tf_op jit(solution)/shard_map/ppermute | solution.py:35
  90.3 1.7 collective-permute-done.3
  92.1 4.6 %all-to-all-done.2 = bf16[16,56,896]{2,1,0:T(8,128)(2,1)S(1)} async-done(((bf16[16,56,896]{2,1,0:T(8,128)(2,1)}), bf16[16,56,896]{2,1,0:T(8,128)(2,1)S(1)}, u32[]{:S(2)}, u32[]{:S(2)}) %all-to-all-start.2) | async-done | bytes 1605664 | tf_op jit(solution)/shard_map/all_to_all | solution.py:39
  96.7 0.9 reduce_sum.38
  97.6 1.7 pad_maximum_fusion.5
  99.3 1.1 constant_dynamic-update-slice_fusion.3
  100.4 1.1 constant_dynamic-update-slice_fusion.2
  101.5 1.3 convolution_convert_fusion
  103.0 22.0 %all_to_all.31 = bf16[16,32,896]{2,1,0:T(8,128)(2,1)S(1)} all-to-all(bf16[16,32,896]{2,1,0:T(8,128)(2,1)S(1)} %bitcast.47), channel_id=1, replica_groups=mesh['y'=4,'zl'=2,'zh'=2,'x'=4,'c'=2] {'zh','zl','x'}, dimensions={0} | all-to-all | bytes 1835008 | tf_op jit(solution)/shard_map/all_to_all | solution.py:39
  125.0 0.1 reduce_sum.36
  125.1 1.0 broadcast_in_dim.3
  126.1 3.9 %all-to-all-start.4 = ((bf16[16,32,896]{2,1,0:T(8,128)(2,1)}), bf16[16,32,896]{2,1,0:T(8,128)(2,1)S(1)}, u32[]{:S(2)}, u32[]{:S(2)}) async-start(bf16[16,32,896]{2,1,0:T(8,128)(2,1)} %broadcast_in_dim.3), calls=%async_computation.4 | async-start | bytes 1835008 | tf_op jit(solution)/shard_map/all_to_all | solution.py:39
  130.1 1.4 pad_maximum_fusion.2
  131.5 2.0 pad_maximum_fusion
  133.5 14.8 %all-to-all-done.4 = bf16[16,32,896]{2,1,0:T(8,128)(2,1)S(1)} async-done(((bf16[16,32,896]{2,1,0:T(8,128)(2,1)}), bf16[16,32,896]{2,1,0:T(8,128)(2,1)S(1)}, u32[]{:S(2)}, u32[]{:S(2)}) %all-to-all-start.4) | async-done | bytes 917536 | tf_op jit(solution)/shard_map/all_to_all | solution.py:39
  148.4 4.6 %fusion.12 = f32[896,1152]{1,0:T(8,128)} fusion(bf16[448,896]{1,0:T(8,128)(2,1)S(1)} %bitcast.50, bf16[448,1152]{1,0:T(8,128)(2,1)} %copy-done.6), kind=kOutput, calls=%fused_computation.34 | convolution fusion | flops 924844032 | bytes 5963776 | tf_op jit(solution)/shard_map/dot_general | solution.py:28
  153.0 2.7 %all-gather.2.cloned.1.call-done = bf16[1408,896]{1,0:T(8,128)(2,1)} async-done(((bf16[88,896]{1,0:T(8,128)(2,1)}), bf16[1408,896]{1,0:T(8,128)(2,1)}) %all-gather.2.cloned.1.call-update) | async-done | bytes 2523152 | tf_op jit(solution)/shard_map/all_gather | solution.py:82
  155.7 7.8 %convolution_add_fusion = f32[896,1152]{1,0:T(8,128)S(1)} fusion(f32[896,1152]{1,0:T(8,128)} %fusion.12, bf16[1408,896]{1,0:T(8,128)(2,1)} %all-gather.2.cloned.1.call-done, bf16[1408,1152]{1,0:T(8,128)(2,1)} %bitcast.37), kind=kOutput, calls=%fused_computation | convolution fusion | flops 2907684864 | bytes 14024704 | tf_op jit(solution)/shard_map/dot_general | solution.py:28
  163.5 0.1 slice.61
  163.6 2.4 collective-permute-start.5
  166.0 2.3 collective-permute-done.5
  168.3 0.5 fusion.4
  168.8 0.5 collective-permute-start.7
  169.3 1.0 collective-permute-start.6
  170.4 22.5 %collective-permute-done.7 = bf16[448,1152]{1,0:T(8,128)(2,1)S(1)} collective-permute-done((bf16[448,1152]{1,0:T(8,128)(2,1)S(1)}, bf16[448,1152]{1,0:T(8,128)(2,1)S(1)}, u32[]{:S(2)}, u32[]{:S(2)}) %collective-permute-start.7) | collective-permute-done | bytes 1032224 | tf_op jit(solution)/shard_map/ppermute | solution.py:35
  192.9 1.7 collective-permute-start.9
  194.6 0.3 collective-permute-start.8
  194.9 0.2 pad_maximum_fusion.3
  195.1 0.2 pad_maximum_fusion.1
  195.4 1.4 copy-done
  196.8 3.8 %fusion.13 = f32[896,1152]{1,0:T(8,128)S(1)} fusion(bf16[1408,896]{1,0:T(8,128)(2,1)S(1)} %copy-done, bf16[1408,1152]{1,0:T(8,128)(2,1)S(1)} %bitcast.48), kind=kOutput, calls=%fused_computation.35 | convolution fusion | flops 2906652672 | bytes 9895936 | tf_op jit(solution)/shard_map/dot_general | solution.py:28
  200.6 4.4 %collective-permute-done.9 = bf16[224,1152]{1,0:T(8,128)(2,1)S(1)} collective-permute-done((bf16[224,1152]{1,0:T(8,128)(2,1)S(1)}, bf16[224,1152]{1,0:T(8,128)(2,1)S(1)}, u32[]{:S(2)}, u32[]{:S(2)}) %collective-permute-start.9) | collective-permute-done | bytes 516128 | tf_op jit(solution)/shard_map/ppermute | solution.py:35
  205.0 2.9 %collective-permute-done.8 = bf16[224,1152]{1,0:T(8,128)(2,1)S(1)} collective-permute-done((bf16[224,1152]{1,0:T(8,128)(2,1)S(1)}, bf16[224,1152]{1,0:T(8,128)(2,1)S(1)}, u32[]{:S(2)}, u32[]{:S(2)}) %collective-permute-start.8) | collective-permute-done | bytes 516128 | tf_op jit(solution)/shard_map/ppermute | solution.py:35
  207.9 1.4 fusion.7
  209.3 0.4 add.29
  209.7 0.1 slice.60
  209.8 2.5 %collective-permute-start.10 = (bf16[448,1152]{1,0:T(8,128)(2,1)S(1)}, bf16[448,1152]{1,0:T(8,128)(2,1)S(1)}, u32[]{:S(2)}, u32[]{:S(2)}) collective-permute-start(bf16[448,1152]{1,0:T(8,128)(2,1)S(1)} %slice.60), channel_id=1, source_target_pairs={{0,1},{1,0},{2,3},{3,2},{4,5},{5,4},{6,7},{7,6},{8,9},{9,8},{10,11... | collective-permute-start | bytes 3096584 | tf_op jit(solution)/shard_map/ppermute | solution.py:35
  212.3 2.3 collective-permute-done.10
  214.6 0.5 fusion.2
  215.1 0.3 reshape.52
  215.3 21.8 %all_to_all.32 = bf16[16,28,1152]{2,1,0:T(8,128)(2,1)S(1)} all-to-all(bf16[16,28,1152]{2,1,0:T(8,128)(2,1)S(1)} %reshape.52), channel_id=1, replica_groups=mesh['y'=4,'zl'=2,'zh'=2,'x'=4,'c'=2] {'zh','zl','x'}, dimensions={0} | all-to-all | bytes 2064384 | tf_op jit(solution)/shard_map/all_to_all | solution.py:39
  237.1 0.3 copy.6
  237.5 1.2 copy.8
  (28 shorter events, 0.7 us)
Async XLA Ops:
  34.1 5.0 %collective-permute-start = (bf16[448,1152]{1,0:T(8,128)(2,1)S(1)}, bf16[448,1152]{1,0:T(8,128)(2,1)S(1)}, u32[]{:S(2)}, u32[]{:S(2)}) collective-permute-start(bf16[448,1152]{1,0:T(8,128)(2,1)S(1)} %reshape.42), channel_id=1, source_target_pairs={{0,1},{1,0},{2,3},{3,2},{4,5},{5,4},{6,7},{7,6},{8,9},{9,8},{10,11... | collective-permute-start | bytes 3096584 | tf_op jit(solution)/shard_map/ppermute | solution.py:35
  36.3 24.9 %collective-permute-start.2 = (bf16[448,1152]{1,0:T(8,128)(2,1)S(1)}, bf16[448,1152]{1,0:T(8,128)(2,1)S(1)}, u32[]{:S(2)}, u32[]{:S(2)}) collective-permute-start(bf16[448,1152]{1,0:T(8,128)(2,1)S(1)} %reshape.42), channel_id=1, source_target_pairs={{0,96},{1,97},{2,98},{3,99},{4,100},{5,101},{6,102},{7,103},{8,104... | collective-permute-start | bytes 3096584 | tf_op jit(solution)/shard_map/ppermute | solution.py:35
  39.0 25.4 %collective-permute-start.1 = (bf16[448,1152]{1,0:T(8,128)(2,1)S(1)}, bf16[448,1152]{1,0:T(8,128)(2,1)}, u32[]{:S(2)}, u32[]{:S(2)}) collective-permute-start(bf16[448,1152]{1,0:T(8,128)(2,1)S(1)} %reshape.42), channel_id=1, source_target_pairs={{0,32},{1,33},{2,34},{3,35},{4,36},{5,37},{6,38},{7,39},{8,40},{9,... | collective-permute-start | bytes 3096584 | tf_op jit(solution)/shard_map/ppermute | solution.py:35
  39.3 1.4 copy-start.3
  41.7 22.7 %all-to-all-start.1 = ((bf16[16,32,896]{2,1,0:T(8,128)(2,1)}), bf16[16,32,896]{2,1,0:T(8,128)(2,1)S(1)}, u32[]{:S(2)}, u32[]{:S(2)}) async-start(bf16[16,32,896]{2,1,0:T(8,128)(2,1)} %bitcast.2), calls=%async_computation.1 | async-start | bytes 1835008 | tf_op jit(solution)/shard_map/all_to_all | solution.py:39
  61.2 6.6 %copy-start.1 = (bf16[448,1152]{1,0:T(8,128)(2,1)}, bf16[448,1152]{1,0:T(8,128)(2,1)S(1)}, u32[]{:S(2)}) copy-start(bf16[448,1152]{1,0:T(8,128)(2,1)S(1)} %collective-permute-done.2) | copy-start | bytes 3096580
  64.4 3.4 %copy-start.4 = (bf16[896,1152]{1,0:T(8,128)(2,1)S(1)}, bf16[896,1152]{1,0:T(8,128)(2,1)}, u32[]{:S(2)}) copy-start(bf16[896,1152]{1,0:T(8,128)(2,1)} %copy-done.3) | copy-start | bytes 6193156
  70.4 26.3 %all-to-all-start.2 = ((bf16[16,56,896]{2,1,0:T(8,128)(2,1)}), bf16[16,56,896]{2,1,0:T(8,128)(2,1)S(1)}, u32[]{:S(2)}, u32[]{:S(2)}) async-start(bf16[16,56,896]{2,1,0:T(8,128)(2,1)} %bitcast.40), calls=%async_computation.2 | async-start | bytes 3211264 | tf_op jit(solution)/shard_map/all_to_all | solution.py:39
  74.1 81.6 %all-gather.2.cloned.1.call-start = ((), (), s32[]{:S(2)}) async-start(), calls=%async_computation.6 | async-start | bytes 2680832 | tf_op jit(solution)/shard_map/all_gather | solution.py:82
  78.0 12.4 %collective-permute-start.4 = (bf16[224,1152]{1,0:T(8,128)(2,1)}, bf16[224,1152]{1,0:T(8,128)(2,1)}, u32[]{:S(2)}, u32[]{:S(2)}) collective-permute-start(bf16[224,1152]{1,0:T(8,128)(2,1)} %slice.33), channel_id=1, source_target_pairs={{0,96},{1,97},{2,98},{3,99},{4,100},{5,101},{6,102},{7,103},{8,104... | collective-permute-start | bytes 1548296 | tf_op jit(solution)/shard_map/ppermute | solution.py:35
  78.5 13.6 %collective-permute-start.3 = (bf16[224,1152]{1,0:T(8,128)(2,1)}, bf16[224,1152]{1,0:T(8,128)(2,1)}, u32[]{:S(2)}, u32[]{:S(2)}) collective-permute-start(bf16[224,1152]{1,0:T(8,128)(2,1)} %slice.32), channel_id=1, source_target_pairs={{0,32},{1,33},{2,34},{3,35},{4,36},{5,37},{6,38},{7,39},{8,40},{9,... | collective-permute-start | bytes 1548296 | tf_op jit(solution)/shard_map/ppermute | solution.py:35
  97.6 3.9 %copy-start.5 = (bf16[896,1152]{1,0:T(8,128)(2,1)S(1)}, bf16[896,1152]{1,0:T(8,128)(2,1)}, u32[]{:S(2)}) copy-start(bf16[896,1152]{1,0:T(8,128)(2,1)} %copy-done.3) | copy-start | bytes 6193156
  101.5 1.4 copy-start.6
  126.1 4.1 %copy-start.2 = (bf16[448,1152]{1,0:T(8,128)(2,1)S(1)}, bf16[448,1152]{1,0:T(8,128)(2,1)}, u32[]{:S(2)}) copy-start(bf16[448,1152]{1,0:T(8,128)(2,1)} %copy-done.1) | copy-start | bytes 3096580
  126.1 22.2 %all-to-all-start.4 = ((bf16[16,32,896]{2,1,0:T(8,128)(2,1)}), bf16[16,32,896]{2,1,0:T(8,128)(2,1)S(1)}, u32[]{:S(2)}, u32[]{:S(2)}) async-start(bf16[16,32,896]{2,1,0:T(8,128)(2,1)} %broadcast_in_dim.3), calls=%async_computation.4 | async-start | bytes 1835008 | tf_op jit(solution)/shard_map/all_to_all | solution.py:39
  163.6 4.7 %collective-permute-start.5 = (bf16[448,1152]{1,0:T(8,128)(2,1)S(1)}, bf16[448,1152]{1,0:T(8,128)(2,1)S(1)}, u32[]{:S(2)}, u32[]{:S(2)}) collective-permute-start(bf16[448,1152]{1,0:T(8,128)(2,1)S(1)} %slice.61), channel_id=1, source_target_pairs={{0,1},{1,0},{2,3},{3,2},{4,5},{5,4},{6,7},{7,6},{8,9},{9,8},{10,11... | collective-permute-start | bytes 3096584 | tf_op jit(solution)/shard_map/ppermute | solution.py:35
  168.8 24.1 %collective-permute-start.7 = (bf16[448,1152]{1,0:T(8,128)(2,1)S(1)}, bf16[448,1152]{1,0:T(8,128)(2,1)S(1)}, u32[]{:S(2)}, u32[]{:S(2)}) collective-permute-start(bf16[448,1152]{1,0:T(8,128)(2,1)S(1)} %fusion.4), channel_id=1, source_target_pairs={{0,96},{1,97},{2,98},{3,99},{4,100},{5,101},{6,102},{7,103},{8,104... | collective-permute-start | bytes 3096584 | tf_op jit(solution)/shard_map/ppermute | solution.py:35
  169.3 25.3 %collective-permute-start.6 = (bf16[448,1152]{1,0:T(8,128)(2,1)S(1)}, bf16[448,1152]{1,0:T(8,128)(2,1)S(1)}, u32[]{:S(2)}, u32[]{:S(2)}) collective-permute-start(bf16[448,1152]{1,0:T(8,128)(2,1)S(1)} %fusion.4), channel_id=1, source_target_pairs={{0,32},{1,33},{2,34},{3,35},{4,36},{5,37},{6,38},{7,39},{8,40},{9,... | collective-permute-start | bytes 3096584 | tf_op jit(solution)/shard_map/ppermute | solution.py:35
  192.9 12.1 %collective-permute-start.9 = (bf16[224,1152]{1,0:T(8,128)(2,1)S(1)}, bf16[224,1152]{1,0:T(8,128)(2,1)S(1)}, u32[]{:S(2)}, u32[]{:S(2)}) collective-permute-start(bf16[224,1152]{1,0:T(8,128)(2,1)S(1)} %slice.46), channel_id=1, source_target_pairs={{0,96},{1,97},{2,98},{3,99},{4,100},{5,101},{6,102},{7,103},{8,104... | collective-permute-start | bytes 1548296 | tf_op jit(solution)/shard_map/ppermute | solution.py:35
  194.6 13.3 %collective-permute-start.8 = (bf16[224,1152]{1,0:T(8,128)(2,1)S(1)}, bf16[224,1152]{1,0:T(8,128)(2,1)S(1)}, u32[]{:S(2)}, u32[]{:S(2)}) collective-permute-start(bf16[224,1152]{1,0:T(8,128)(2,1)S(1)} %slice.45), channel_id=1, source_target_pairs={{0,32},{1,33},{2,34},{3,35},{4,36},{5,37},{6,38},{7,39},{8,40},{9,... | collective-permute-start | bytes 1548296 | tf_op jit(solution)/shard_map/ppermute | solution.py:35
  195.1 1.7 copy-start
  209.8 4.7 %collective-permute-start.10 = (bf16[448,1152]{1,0:T(8,128)(2,1)S(1)}, bf16[448,1152]{1,0:T(8,128)(2,1)S(1)}, u32[]{:S(2)}, u32[]{:S(2)}) collective-permute-start(bf16[448,1152]{1,0:T(8,128)(2,1)S(1)} %slice.60), channel_id=1, source_target_pairs={{0,1},{1,0},{2,3},{3,2},{4,5},{5,4},{6,7},{7,6},{8,9},{9,8},{10,11... | collective-permute-start | bytes 3096584 | tf_op jit(solution)/shard_map/ppermute | solution.py:35
Sparse Core Ops, SparseCore 0:
  99.5 56.1 all-gather.1

commit v4 on v3

--- a/solution.py
+++ b/solution.py
@@ -22,17 +22,23 @@
 OWN_STRIP = 32
 NEAR_STRIP = 56
 FAR_STRIP = 32
+PART = 48
 
 
 def dot(a, b, dims):
     return lax.dot_general(a, b, (dims, ((), ())), preferred_element_type=jnp.float32)
 
 
-def move(a, dy=0, dc=0):
+def move(a, dy=0, dz=0, dx=0, dc=0):
     index = np.arange(math.prod(SIZES)).reshape(SIZES)
-    target = np.roll(np.roll(index, -dy, axis=0), -dc, axis=4)
-    pairs = [(int(s), int(t)) for s, t in zip(index.ravel(), target.ravel())]
+    by_place = index.transpose(0, 2, 1, 3, 4).reshape(4, 4, 4, 2)
+    target = np.roll(by_place, (-dy, -dz, -dx, -dc), axis=(0, 1, 2, 3))
+    pairs = [(int(s), int(t)) for s, t in zip(by_place.ravel(), target.ravel())]
     return lax.ppermute(a, AXES, pairs)
+
+
+def gather_ring(a, axis):
+    return jnp.stack([a, move(a, **{axis: -1}), move(a, **{axis: 2}), move(a, **{axis: 1})])
 
 
 def trade(a):
@@ -77,22 +83,34 @@
     far_low, far_high = forward(below, above)
     near = jnp.concatenate([columns(below), columns(above)])
     near_terms = terms_of_strips(near, NEAR_STRIP)
-    near_terms, far_low, far_high = lax.optimization_barrier((near_terms, far_low, far_high))
     strip = jnp.concatenate([strip_of(own_terms), strip_of(near_terms)])
-    gram = lax.all_gather(strip, PLANE, axis=0, tiled=True)
+    strip, far_low, far_high = lax.optimization_barrier((strip, far_low, far_high))
+    gram = [
+        gather_ring(gather_ring(strip[:PART], "dx"), "dz"),
+        gather_ring(gather_ring(strip[PART:], "dz"), "dx"),
+    ]
     far = jnp.concatenate([far_low, far_high])
     strip = strip_of(terms_of_strips(columns(far), FAR_STRIP))
     gram_far = trade(jnp.broadcast_to(strip, (16,) + strip.shape)).reshape(-1, M // 4)[:BAND]
-    panel = in_strips(tile, below, above)
+    place = (lax.axis_index(("zh", "zl")), lax.axis_index("x"))
+    panel = in_strips(tile, below, above).reshape(4, 4, -1, PANEL)
+    panel = jnp.roll(panel, (-place[0], -place[1]), (0, 1))
+    panel = [panel[:, :, :PART].reshape(-1, PANEL)] + [
+        panel[:, :, PART:].transpose(1, 0, 2, 3).reshape(-1, PANEL)
+    ]
 
     wide_tile = tile.astype(jnp.float32)
     cubed, gram, panel = lax.optimization_barrier((dot(gram_far, far, ((0,), (0,))), gram, panel))
-    cubed = cubed + dot(gram, panel, ((0,), (0,)))
+    for part, rows in zip(gram, panel):
+        cubed = cubed + dot(part.reshape(-1, M // 4), rows, ((0,), (0,)))
     inner = CUBIC_COEF * wide_tile + QUINTIC_COEF * with_other_core(cubed)
     inner = inner.astype(jnp.bfloat16)
 
     below, above = move(inner, dy=1), move(inner, dy=-1)
     far_low, far_high = forward(below, above)
+    gram = jnp.concatenate([gram[0], gram[1].transpose(1, 0, 2, 3)], axis=2)
+    gram = jnp.roll(gram, place, (0, 1)).reshape(-1, M // 4)
+    gram, below, above = lax.optimization_barrier((gram, below, above))
     total = dot(gram, in_strips(inner, below, above), ((0,), (0,)))
     total, far_low, far_high = lax.optimization_barrier((total, far_low, far_high))
     total = total + dot(gram_far, jnp.concatenate([far_low, far_high]), ((0,), (0,)))

time: 246 us -> 244 us (level)
  starting transfers between devices: 26.2 us -> 52 us
  blocking collectives: 69.4 us -> 47.8 us
  other arithmetic: 9.85 us -> 23.3 us
  between operations: 13.7 us -> 0.56 us
  waiting for transfers between devices: 87.5 us -> 79.1 us
  local copies, waits for them, and re-layouts: 14 us -> 20.3 us
  matrix products: 24.9 us -> 19.6 us
    all_to_all x3 -> x2, blocking collectives: 69.4 us -> 47.8 us  [trade(): return lax.all_to_all(a, PLANE, split_axis=0, concat_axis=0, tiled=True)]
    ppermute x11 -> x23, starting transfers between devices: 14.8 us -> 34.8 us  [move(): return lax.ppermute(a, AXES, pairs)]
    concatenate x0 -> x4, other arithmetic: none -> 10.8 us  [the longest x2 7.95 us: body(): panel = jnp.roll(panel, (-place[0], -place[1]), (0, 1))]
    all_to_all x3 -> x4, waiting for transfers between devices: 19.5 us -> 11.7 us  [trade(): return lax.all_to_all(a, PLANE, split_axis=0, concat_axis=0, tiled=True)]
    all_to_all x3 -> x4, starting transfers between devices: 11.3 us -> 17.2 us  [trade(): return lax.all_to_all(a, PLANE, split_axis=0, concat_axis=0, tiled=True)]
    dot_general x8 -> x9, matrix products: 24.9 us -> 19.6 us  [dot(): lax.dot_general(a, b, (dims, ((), ())), preferred_element_type=jnp.float32)]
    another operation x0 -> x4, other arithmetic: none -> 4.15 us  [gather_ring(): jnp.stack([a, move(a, **{axis: -1}), move(a, **{axis: 2}), move(a, **{axi...]
    all_gather x1 -> x0, waiting for transfers between devices: 2.72 us -> none  [body(): gram = lax.all_gather(strip, PLANE, axis=0, tiled=True)]
  transfers between devices with their start and end apart: 15 -> 27, of which waited for: 12 -> 12; matrix products, arithmetic and copies ran while one was open for 10% -> 15% of each run, Pallas kernels for 0% -> 0%
where the time goes in v4:
time: 244 us; the launch traced here: 243 us
  waiting for transfers between devices  79.1 us (32%)
  starting transfers between devices  52 us (21%)
  blocking collectives  47.8 us (20%)
  other arithmetic  23.3 us (10%)
  local copies, waits for them, and re-layouts  20.3 us (8%)
  matrix products  19.6 us (8%)
    ppermute x23, waiting for transfers between devices, move(): return lax.ppermute(a, AXES, pairs)  67.4 us
    all_to_all x2, blocking collectives, trade(): return lax.all_to_all(a, PLANE, split_axis=0, concat_axis=0, tiled=True)  47.8 us
    ppermute x23, starting transfers between devices, move(): return lax.ppermute(a, AXES, pairs)  34.8 us
    dot_general x9, matrix products, dot(): lax.dot_general(a, b, (dims, ((), ())), preferred_element_type=jnp.float32)  19.6 us
    all_to_all x4, starting transfers between devices, trade(): return lax.all_to_all(a, PLANE, split_axis=0, concat_axis=0, tiled=True)  17.2 us
    all_to_all x4, waiting for transfers between devices, trade(): return lax.all_to_all(a, PLANE, split_axis=0, concat_axis=0, tiled=True)  11.7 us
    concatenate x2, other arithmetic, body(): panel = jnp.roll(panel, (-place[0], -place[1]), (0, 1))  7.95 us
  transfers between devices with their start and end apart: 27, of which 12 were waited for; matrix products, arithmetic and copies ran while one was open for 15% of the time, Pallas kernels for 0%

profile of v4, /device:TPU:1, one launch (start us, length us, event | category | flops | bytes accessed | tf_op | source)
XLA Modules:
  0.0 242.7 jit_solution(1319852083189162510)
XLA Ops:
  0.0 1.4 copy.13
  1.7 25.6 %all_to_all.30 = bf16[16,28,1152]{2,1,0:T(8,128)(2,1)S(1)} all-to-all(bf16[16,28,1152]{2,1,0:T(8,128)(2,1)S(1)} %bitcast.79), channel_id=1, replica_groups=mesh['y'=4,'zl'=2,'zh'=2,'x'=4,'c'=2] {'zh','zl','x'}, dimensions={0} | all-to-all | bytes 2064384 | tf_op jit(solution)/shard_map/all_to_all | solution.py:45
  27.6 2.2 collective-permute-start
  29.7 2.7 %collective-permute-start.2 = (bf16[448,1152]{1,0:T(8,128)(2,1)S(1)}, bf16[448,1152]{1,0:T(8,128)(2,1)S(1)}, u32[]{:S(2)}, u32[]{:S(2)}) collective-permute-start(bf16[448,1152]{1,0:T(8,128)(2,1)S(1)} %reshape.54), channel_id=1, source_target_pairs={{0,96},{1,97},{2,98},{3,99},{4,100},{5,101},{6,102},{7,103},{16,11... | collective-permute-start | bytes 3096584 | tf_op jit(solution)/shard_map/ppermute | solution.py:37
  32.8 1.3 fusion.14
  34.1 1.0 pad.14
  35.1 3.6 %all-to-all-start.1 = ((bf16[16,32,896]{2,1,0:T(8,128)(2,1)}), bf16[16,32,896]{2,1,0:T(8,128)(2,1)S(1)}, u32[]{:S(2)}, u32[]{:S(2)}) async-start(bf16[16,32,896]{2,1,0:T(8,128)(2,1)} %bitcast.2), calls=%async_computation.1 | async-start | bytes 1835008 | tf_op jit(solution)/shard_map/all_to_all | solution.py:45
  38.8 15.9 %collective-permute-done.2 = bf16[448,1152]{1,0:T(8,128)(2,1)S(1)} collective-permute-done((bf16[448,1152]{1,0:T(8,128)(2,1)S(1)}, bf16[448,1152]{1,0:T(8,128)(2,1)S(1)}, u32[]{:S(2)}, u32[]{:S(2)}) %collective-permute-start.2) | collective-permute-done | bytes 1032224 | tf_op jit(solution)/shard_map/ppermute | solution.py:37
  54.7 3.2 %collective-permute-done.1 = bf16[448,1152]{1,0:T(8,128)(2,1)} collective-permute-done((bf16[448,1152]{1,0:T(8,128)(2,1)S(1)}, bf16[448,1152]{1,0:T(8,128)(2,1)}, u32[]{:S(2)}, u32[]{:S(2)}) %collective-permute-start.1) | collective-permute-done | bytes 1032224 | tf_op jit(solution)/shard_map/ppermute | solution.py:37
  57.9 3.4 %convolution_convert_fusion.2 = bf16[448,896]{1,0:T(8,128)(2,1)S(1)} fusion(bf16[448,1152]{1,0:T(8,128)(2,1)} %collective-permute-done.1, bf16[896,1152]{1,0:T(8,128)(2,1)} %copy-done.7), kind=kOutput, calls=%fused_computation.41 | convolution fusion | flops 925245440 | bytes 3899392 | tf_op jit(solution)/shard_map/dot_general | solution.py:29
  61.3 1.3 convolution_convert_fusion.1
  62.6 1.4 pad_maximum_fusion.3
  64.0 3.7 %all-to-all-start.2 = ((bf16[16,56,896]{2,1,0:T(8,128)(2,1)}), bf16[16,56,896]{2,1,0:T(8,128)(2,1)S(1)}, u32[]{:S(2)}, u32[]{:S(2)}) async-start(bf16[16,56,896]{2,1,0:T(8,128)(2,1)} %bitcast.73), calls=%async_computation.2 | async-start | bytes 3211264 | tf_op jit(solution)/shard_map/all_to_all | solution.py:45
  67.7 1.1 pad.16
  68.8 1.9 slice.44
  72.8 1.0 collective-permute-start.3
  73.8 1.7 pad_maximum_fusion.1
  75.5 3.1 %fusion.2 = bf16[4,4,88,1152]{3,2,1,0:T(8,128)(2,1)} fusion(s32[]{:T(128)S(6)} %select_n.44, bf16[4,4,32,1152]{3,2,1,0:T(8,128)(2,1)S(1)} %bitcast.77, bf16[4,4,56,1152]{3,2,1,0:T(8,128)(2,1)S(1)} %bitcast.71), kind=kLoop, calls=%fused_computation.16 | loop fusion | flops 12976128 | bytes 6488068 | tf_op jit(solution)/shard_map/jit(_roll_dynamic)/concatenate | solution.py:97
  78.5 11.7 %all-to-all-done.2 = bf16[16,56,896]{2,1,0:T(8,128)(2,1)S(1)} async-done(((bf16[16,56,896]{2,1,0:T(8,128)(2,1)}), bf16[16,56,896]{2,1,0:T(8,128)(2,1)S(1)}, u32[]{:S(2)}, u32[]{:S(2)}) %all-to-all-start.2) | async-done | bytes 1605664 | tf_op jit(solution)/shard_map/all_to_all | solution.py:45
  90.5 1.2 constant_dynamic-update-slice_fusion.3
  92.2 1.3 convolution_convert_fusion
  93.6 1.1 pad.15
  94.6 5.2 %all-to-all-start.3 = ((bf16[16,32,896]{2,1,0:T(8,128)(2,1)}), bf16[16,32,896]{2,1,0:T(8,128)(2,1)S(1)}, u32[]{:S(2)}, u32[]{:S(2)}) async-start(bf16[16,32,896]{2,1,0:T(8,128)(2,1)} %bitcast.4), calls=%async_computation.3 | async-start | bytes 1835008 | tf_op jit(solution)/shard_map/all_to_all | solution.py:45
  99.9 2.9 %collective-permute-start.12 = (bf16[40,896]{1,0:T(8,128)(2,1)S(1)}, bf16[40,896]{1,0:T(8,128)(2,1)S(1)}, u32[]{:S(2)}, u32[]{:S(2)}) collective-permute-start(bf16[40,896]{1,0:T(8,128)(2,1)S(1)} %get-tuple-element.44), channel_id=1, source_target_pairs={{0,8},{1,9},{2,10},{3,11},{4,12},{5,13},{6,14},{7,15},{16,24},{17,... | collective-permute-start | bytes 215048 | tf_op jit(solution)/shard_map/ppermute | solution.py:37
  104.3 2.8 %collective-permute-start.6 = (bf16[48,896]{1,0:T(8,128)(2,1)S(1)}, bf16[48,896]{1,0:T(8,128)(2,1)S(1)}, u32[]{:S(2)}, u32[]{:S(2)}) collective-permute-start(bf16[48,896]{1,0:T(8,128)(2,1)S(1)} %get-tuple-element.46), channel_id=1, source_target_pairs={{0,4},{1,5},{2,6},{3,7},{4,0},{5,1},{6,2},{7,3},{16,20},{17,21},{1... | collective-permute-start | bytes 258056 | tf_op jit(solution)/shard_map/ppermute | solution.py:37
  108.0 3.1 %collective-permute-done.12 = bf16[40,896]{1,0:T(8,128)(2,1)S(1)} collective-permute-done((bf16[40,896]{1,0:T(8,128)(2,1)S(1)}, bf16[40,896]{1,0:T(8,128)(2,1)S(1)}, u32[]{:S(2)}, u32[]{:S(2)}) %collective-permute-start.12) | collective-permute-done | bytes 71712 | tf_op jit(solution)/shard_map/ppermute | solution.py:37
  111.0 4.0 %collective-permute-start.7 = (bf16[48,896]{1,0:T(8,128)(2,1)S(1)}, bf16[48,896]{1,0:T(8,128)(2,1)S(1)}, u32[]{:S(2)}, u32[]{:S(2)}) collective-permute-start(bf16[48,896]{1,0:T(8,128)(2,1)S(1)} %get-tuple-element.46), channel_id=1, source_target_pairs={{0,2},{1,3},{2,4},{3,5},{4,6},{5,7},{6,0},{7,1},{16,18},{17,19},{1... | collective-permute-start | bytes 258056 | tf_op jit(solution)/shard_map/ppermute | solution.py:37
  115.0 0.9 collective-permute-done.13
  116.7 3.2 %collective-permute-start.15 = (bf16[4,40,896]{2,1,0:T(8,128)(2,1)}, bf16[4,40,896]{2,1,0:T(8,128)(2,1)}, u32[]{:S(2)}, u32[]{:S(2)}) collective-permute-start(bf16[4,40,896]{2,1,0:T(8,128)(2,1)} %get-tuple-element.42), channel_id=1, source_target_pairs={{0,4},{1,5},{2,6},{3,7},{4,0},{5,1},{6,2},{7,3},{16,20},{17,21},{1... | collective-permute-start | bytes 860168 | tf_op jit(solution)/shard_map/ppermute | solution.py:37
  119.9 4.9 %fusion = bf16[4,4,88,1152]{3,2,1,0:T(8,128)(2,1)} fusion(s32[]{:T(128)S(6)} %select_n.46, bf16[4,4,88,1152]{3,2,1,0:T(8,128)(2,1)} %fusion.2), kind=kLoop, calls=%fused_computation.14 | loop fusion | flops 1622016 | bytes 6488068 | tf_op jit(solution)/shard_map/jit(_roll_dynamic)/concatenate | solution.py:97
  125.4 0.9 collective-permute-start.16
  127.7 1.5 collective-permute-start.8
  129.4 1.0 broadcast_in_dim.2
  130.4 4.6 %all-to-all-start.4 = ((bf16[16,32,896]{2,1,0:T(8,128)(2,1)}), bf16[16,32,896]{2,1,0:T(8,128)(2,1)}, u32[]{:S(2)}, u32[]{:S(2)}) async-start(bf16[16,32,896]{2,1,0:T(8,128)(2,1)} %broadcast_in_dim.2), calls=%async_computation.4 | async-start | bytes 1835008 | tf_op jit(solution)/shard_map/all_to_all | solution.py:45
  135.0 1.4 collective-permute-start.10
  136.4 1.5 slice_bitcast_fusion
  137.9 1.2 copy.10
  139.1 1.3 pad_maximum_fusion.5
  140.5 10.5 %collective-permute-done.8 = bf16[4,48,896]{2,1,0:T(8,128)(2,1)S(1)} collective-permute-done((bf16[4,48,896]{2,1,0:T(8,128)(2,1)S(1)}, bf16[4,48,896]{2,1,0:T(8,128)(2,1)S(1)}, u32[]{:S(2)}, u32[]{:S(2)}) %collective-permute-start.8) | collective-permute-done | bytes 344096 | tf_op jit(solution)/shard_map/ppermute | solution.py:37
  150.9 3.4 %collective-permute-done.10 = bf16[4,48,896]{2,1,0:T(8,128)(2,1)S(1)} collective-permute-done((bf16[4,48,896]{2,1,0:T(8,128)(2,1)S(1)}, bf16[4,48,896]{2,1,0:T(8,128)(2,1)S(1)}, u32[]{:S(2)}, u32[]{:S(2)}) %collective-permute-start.10) | collective-permute-done | bytes 344096 | tf_op jit(solution)/shard_map/ppermute | solution.py:37
  154.3 1.3 pad_maximum_fusion.4
  155.6 1.2 slice.58
  156.9 2.9 %fusion.22 = f32[896,1152]{1,0:T(8,128)S(1)} fusion(bf16[448,896]{1,0:T(8,128)(2,1)S(1)} %bitcast.85, bf16[448,1152]{1,0:T(8,128)(2,1)} %copy-done.12), kind=kOutput, calls=%fused_computation.63 | convolution fusion | flops 924844032 | bytes 5963776 | tf_op jit(solution)/shard_map/dot_general | solution.py:29
  159.9 2.0 convolution_add_fusion.1
  161.9 2.0 convolution_add_fusion
  164.0 2.3 collective-permute-start.17
  166.4 2.3 collective-permute-done.17
  168.6 1.4 fusion.12
  171.5 1.8 fusion.6
  173.3 1.0 fusion.4
  174.3 1.3 pad.17
  175.6 18.7 %collective-permute-done.19 = bf16[448,1152]{1,0:T(8,128)(2,1)} collective-permute-done((bf16[448,1152]{1,0:T(8,128)(2,1)}, bf16[448,1152]{1,0:T(8,128)(2,1)}, u32[]{:S(2)}, u32[]{:S(2)}) %collective-permute-start.19) | collective-permute-done | bytes 1032224 | tf_op jit(solution)/shard_map/ppermute | solution.py:37
  194.4 1.1 slice.64
  195.5 1.8 collective-permute-start.21
  197.3 1.1 slice.63
  198.5 1.7 pad_maximum_fusion.2
  200.4 3.8 %fusion.23 = f32[896,1152]{1,0:T(8,128)S(1)} fusion(bf16[1408,896]{1,0:T(8,128)(2,1)S(1)} %bitcast.83, bf16[1408,1152]{1,0:T(8,128)(2,1)S(1)} %bitcast.82), kind=kOutput, calls=%fused_computation.64 | convolution fusion | flops 2906652672 | bytes 9895936 | tf_op jit(solution)/shard_map/dot_general | solution.py:29
  204.2 3.4 %collective-permute-done.21 = bf16[224,1152]{1,0:T(8,128)(2,1)S(1)} collective-permute-done((bf16[224,1152]{1,0:T(8,128)(2,1)S(1)}, bf16[224,1152]{1,0:T(8,128)(2,1)S(1)}, u32[]{:S(2)}, u32[]{:S(2)}) %collective-permute-start.21) | collective-permute-done | bytes 516128 | tf_op jit(solution)/shard_map/ppermute | solution.py:37
  207.6 3.8 %collective-permute-done.20 = bf16[224,1152]{1,0:T(8,128)(2,1)S(1)} collective-permute-done((bf16[224,1152]{1,0:T(8,128)(2,1)S(1)}, bf16[224,1152]{1,0:T(8,128)(2,1)S(1)}, u32[]{:S(2)}, u32[]{:S(2)}) %collective-permute-start.20) | collective-permute-done | bytes 516128 | tf_op jit(solution)/shard_map/ppermute | solution.py:37
  211.4 1.4 fusion.15
  213.4 2.5 %collective-permute-start.22 = (bf16[448,1152]{1,0:T(8,128)(2,1)S(1)}, bf16[448,1152]{1,0:T(8,128)(2,1)S(1)}, u32[]{:S(2)}, u32[]{:S(2)}) collective-permute-start(bf16[448,1152]{1,0:T(8,128)(2,1)S(1)} %slice.81), channel_id=1, source_target_pairs={{0,1},{1,0},{2,3},{3,2},{4,5},{5,4},{6,7},{7,6},{16,17},{17,16},{1... | collective-permute-start | bytes 3096584 | tf_op jit(solution)/shard_map/ppermute | solution.py:37
  215.8 2.3 collective-permute-done.22
  218.9 22.2 %all_to_all.31 = bf16[16,28,1152]{2,1,0:T(8,128)(2,1)S(1)} all-to-all(bf16[16,28,1152]{2,1,0:T(8,128)(2,1)S(1)} %reshape.66), channel_id=1, replica_groups=mesh['y'=4,'zl'=2,'zh'=2,'x'=4,'c'=2] {'zh','zl','x'}, dimensions={0} | all-to-all | bytes 2064384 | tf_op jit(solution)/shard_map/all_to_all | solution.py:45
  241.4 1.2 copy.14
  (78 shorter events, 12.4 us)
Async XLA Ops:
  27.6 5.0 %collective-permute-start = (bf16[448,1152]{1,0:T(8,128)(2,1)S(1)}, bf16[448,1152]{1,0:T(8,128)(2,1)S(1)}, u32[]{:S(2)}, u32[]{:S(2)}) collective-permute-start(bf16[448,1152]{1,0:T(8,128)(2,1)S(1)} %reshape.54), channel_id=1, source_target_pairs={{0,1},{1,0},{2,3},{3,2},{4,5},{5,4},{6,7},{7,6},{16,17},{17,16},{1... | collective-permute-start | bytes 3096584 | tf_op jit(solution)/shard_map/ppermute | solution.py:37
  29.7 24.9 %collective-permute-start.2 = (bf16[448,1152]{1,0:T(8,128)(2,1)S(1)}, bf16[448,1152]{1,0:T(8,128)(2,1)S(1)}, u32[]{:S(2)}, u32[]{:S(2)}) collective-permute-start(bf16[448,1152]{1,0:T(8,128)(2,1)S(1)} %reshape.54), channel_id=1, source_target_pairs={{0,96},{1,97},{2,98},{3,99},{4,100},{5,101},{6,102},{7,103},{16,11... | collective-permute-start | bytes 3096584 | tf_op jit(solution)/shard_map/ppermute | solution.py:37
  32.5 25.4 %collective-permute-start.1 = (bf16[448,1152]{1,0:T(8,128)(2,1)S(1)}, bf16[448,1152]{1,0:T(8,128)(2,1)}, u32[]{:S(2)}, u32[]{:S(2)}) collective-permute-start(bf16[448,1152]{1,0:T(8,128)(2,1)S(1)} %reshape.54), channel_id=1, source_target_pairs={{0,32},{1,33},{2,34},{3,35},{4,36},{5,37},{6,38},{7,39},{16,48},{1... | collective-permute-start | bytes 3096584 | tf_op jit(solution)/shard_map/ppermute | solution.py:37
  32.7 1.4 copy-start.7
  35.1 22.7 %all-to-all-start.1 = ((bf16[16,32,896]{2,1,0:T(8,128)(2,1)}), bf16[16,32,896]{2,1,0:T(8,128)(2,1)S(1)}, u32[]{:S(2)}, u32[]{:S(2)}) async-start(bf16[16,32,896]{2,1,0:T(8,128)(2,1)} %bitcast.2), calls=%async_computation.1 | async-start | bytes 1835008 | tf_op jit(solution)/shard_map/all_to_all | solution.py:45
  54.7 6.6 %copy-start.2 = (bf16[448,1152]{1,0:T(8,128)(2,1)}, bf16[448,1152]{1,0:T(8,128)(2,1)S(1)}, u32[]{:S(2)}) copy-start(bf16[448,1152]{1,0:T(8,128)(2,1)S(1)} %collective-permute-done.2) | copy-start | bytes 3096580
  57.9 3.4 %copy-start.8 = (bf16[896,1152]{1,0:T(8,128)(2,1)S(1)}, bf16[896,1152]{1,0:T(8,128)(2,1)}, u32[]{:S(2)}) copy-start(bf16[896,1152]{1,0:T(8,128)(2,1)} %copy-done.7) | copy-start | bytes 6193156
  64.0 26.3 %all-to-all-start.2 = ((bf16[16,56,896]{2,1,0:T(8,128)(2,1)}), bf16[16,56,896]{2,1,0:T(8,128)(2,1)S(1)}, u32[]{:S(2)}, u32[]{:S(2)}) async-start(bf16[16,56,896]{2,1,0:T(8,128)(2,1)} %bitcast.73), calls=%async_computation.2 | async-start | bytes 3211264 | tf_op jit(solution)/shard_map/all_to_all | solution.py:45
  67.7 3.0 %copy-start.3 = (bf16[448,1152]{1,0:T(8,128)(2,1)S(1)}, bf16[448,1152]{1,0:T(8,128)(2,1)}, u32[]{:S(2)}) copy-start(bf16[448,1152]{1,0:T(8,128)(2,1)} %copy-done.2) | copy-start | bytes 3096580
  72.3 3.2 %copy-start.1 = (bf16[512,1152]{1,0:T(8,128)(2,1)S(1)}, bf16[512,1152]{1,0:T(8,128)(2,1)}, u32[]{:S(2)}) copy-start(bf16[512,1152]{1,0:T(8,128)(2,1)} %pad.16) | copy-start | bytes 3538948
  72.3 18.2 %collective-permute-start.4 = (bf16[224,1152]{1,0:T(8,128)(2,1)}, bf16[224,1152]{1,0:T(8,128)(2,1)S(1)}, u32[]{:S(2)}, u32[]{:S(2)}) collective-permute-start(bf16[224,1152]{1,0:T(8,128)(2,1)} %slice.45), channel_id=1, source_target_pairs={{0,96},{1,97},{2,98},{3,99},{4,100},{5,101},{6,102},{7,103},{16,11... | collective-permute-start | bytes 1548296 | tf_op jit(solution)/shard_map/ppermute | solution.py:37
  72.8 17.7 %collective-permute-start.3 = (bf16[224,1152]{1,0:T(8,128)(2,1)}, bf16[224,1152]{1,0:T(8,128)(2,1)}, u32[]{:S(2)}, u32[]{:S(2)}) collective-permute-start(bf16[224,1152]{1,0:T(8,128)(2,1)} %slice.44), channel_id=1, source_target_pairs={{0,32},{1,33},{2,34},{3,35},{4,36},{5,37},{6,38},{7,39},{16,48},{1... | collective-permute-start | bytes 1548296 | tf_op jit(solution)/shard_map/ppermute | solution.py:37
  75.5 15.0 %copy-start.13 = (bf16[32,896]{1,0:T(8,128)(2,1)S(1)}, bf16[32,896]{1,0:T(8,128)(2,1)}, u32[]{:S(2)}) copy-start(bf16[32,896]{1,0:T(8,128)(2,1)} %reduce_sum.36) | copy-start | bytes 172036
  90.5 1.7 copy-start.9
  92.2 1.3 copy-start.12
  94.6 34.6 %all-to-all-start.3 = ((bf16[16,32,896]{2,1,0:T(8,128)(2,1)}), bf16[16,32,896]{2,1,0:T(8,128)(2,1)S(1)}, u32[]{:S(2)}, u32[]{:S(2)}) async-start(bf16[16,32,896]{2,1,0:T(8,128)(2,1)} %bitcast.4), calls=%async_computation.3 | async-start | bytes 1835008 | tf_op jit(solution)/shard_map/all_to_all | solution.py:45
  99.9 11.2 %collective-permute-start.12 = (bf16[40,896]{1,0:T(8,128)(2,1)S(1)}, bf16[40,896]{1,0:T(8,128)(2,1)S(1)}, u32[]{:S(2)}, u32[]{:S(2)}) collective-permute-start(bf16[40,896]{1,0:T(8,128)(2,1)S(1)} %get-tuple-element.44), channel_id=1, source_target_pairs={{0,8},{1,9},{2,10},{3,11},{4,12},{5,13},{6,14},{7,15},{16,24},{17,... | collective-permute-start | bytes 215048 | tf_op jit(solution)/shard_map/ppermute | solution.py:37
  102.8 12.2 %collective-permute-start.11 = (bf16[40,896]{1,0:T(8,128)(2,1)S(1)}, bf16[40,896]{1,0:T(8,128)(2,1)S(1)}, u32[]{:S(2)}, u32[]{:S(2)}) collective-permute-start(bf16[40,896]{1,0:T(8,128)(2,1)S(1)} %get-tuple-element.44), channel_id=1, source_target_pairs={{0,24},{1,25},{2,26},{3,27},{4,28},{5,29},{6,30},{7,31},{16,0},{17... | collective-permute-start | bytes 215048 | tf_op jit(solution)/shard_map/ppermute | solution.py:37
  103.7 12.3 %collective-permute-start.13 = (bf16[40,896]{1,0:T(8,128)(2,1)S(1)}, bf16[40,896]{1,0:T(8,128)(2,1)S(1)}, u32[]{:S(2)}, u32[]{:S(2)}) collective-permute-start(bf16[40,896]{1,0:T(8,128)(2,1)S(1)} %get-tuple-element.44), channel_id=1, source_target_pairs={{0,16},{1,17},{2,18},{3,19},{4,20},{5,21},{6,22},{7,23},{16,8},{17... | collective-permute-start | bytes 215048 | tf_op jit(solution)/shard_map/ppermute | solution.py:37
  104.3 21.1 %collective-permute-start.6 = (bf16[48,896]{1,0:T(8,128)(2,1)S(1)}, bf16[48,896]{1,0:T(8,128)(2,1)S(1)}, u32[]{:S(2)}, u32[]{:S(2)}) collective-permute-start(bf16[48,896]{1,0:T(8,128)(2,1)S(1)} %get-tuple-element.46), channel_id=1, source_target_pairs={{0,4},{1,5},{2,6},{3,7},{4,0},{5,1},{6,2},{7,3},{16,20},{17,21},{1... | collective-permute-start | bytes 258056 | tf_op jit(solution)/shard_map/ppermute | solution.py:37
  107.1 19.2 %collective-permute-start.5 = (bf16[48,896]{1,0:T(8,128)(2,1)S(1)}, bf16[48,896]{1,0:T(8,128)(2,1)S(1)}, u32[]{:S(2)}, u32[]{:S(2)}) collective-permute-start(bf16[48,896]{1,0:T(8,128)(2,1)S(1)} %get-tuple-element.46), channel_id=1, source_target_pairs={{0,6},{1,7},{2,0},{3,1},{4,2},{5,3},{6,4},{7,5},{16,22},{17,23},{1... | collective-permute-start | bytes 258056 | tf_op jit(solution)/shard_map/ppermute | solution.py:37
  111.0 15.3 %collective-permute-start.7 = (bf16[48,896]{1,0:T(8,128)(2,1)S(1)}, bf16[48,896]{1,0:T(8,128)(2,1)S(1)}, u32[]{:S(2)}, u32[]{:S(2)}) collective-permute-start(bf16[48,896]{1,0:T(8,128)(2,1)S(1)} %get-tuple-element.46), channel_id=1, source_target_pairs={{0,2},{1,3},{2,4},{3,5},{4,6},{5,7},{6,0},{7,1},{16,18},{17,19},{1... | collective-permute-start | bytes 258056 | tf_op jit(solution)/shard_map/ppermute | solution.py:37
  116.7 18.3 %collective-permute-start.15 = (bf16[4,40,896]{2,1,0:T(8,128)(2,1)}, bf16[4,40,896]{2,1,0:T(8,128)(2,1)}, u32[]{:S(2)}, u32[]{:S(2)}) collective-permute-start(bf16[4,40,896]{2,1,0:T(8,128)(2,1)} %get-tuple-element.42), channel_id=1, source_target_pairs={{0,4},{1,5},{2,6},{3,7},{4,0},{5,1},{6,2},{7,3},{16,20},{17,21},{1... | collective-permute-start | bytes 860168 | tf_op jit(solution)/shard_map/ppermute | solution.py:37
  124.8 14.3 %collective-permute-start.14 = (bf16[4,40,896]{2,1,0:T(8,128)(2,1)}, bf16[4,40,896]{2,1,0:T(8,128)(2,1)}, u32[]{:S(2)}, u32[]{:S(2)}) collective-permute-start(bf16[4,40,896]{2,1,0:T(8,128)(2,1)} %get-tuple-element.42), channel_id=1, source_target_pairs={{0,6},{1,7},{2,0},{3,1},{4,2},{5,3},{6,4},{7,5},{16,22},{17,23},{1... | collective-permute-start | bytes 860168 | tf_op jit(solution)/shard_map/ppermute | solution.py:37
  125.4 13.8 %collective-permute-start.16 = (bf16[4,40,896]{2,1,0:T(8,128)(2,1)}, bf16[4,40,896]{2,1,0:T(8,128)(2,1)}, u32[]{:S(2)}, u32[]{:S(2)}) collective-permute-start(bf16[4,40,896]{2,1,0:T(8,128)(2,1)} %get-tuple-element.42), channel_id=1, source_target_pairs={{0,2},{1,3},{2,4},{3,5},{4,6},{5,7},{6,0},{7,1},{16,18},{17,19},{1... | collective-permute-start | bytes 860168 | tf_op jit(solution)/shard_map/ppermute | solution.py:37
  127.1 13.4 %collective-permute-start.9 = (bf16[4,48,896]{2,1,0:T(8,128)(2,1)S(1)}, bf16[4,48,896]{2,1,0:T(8,128)(2,1)S(1)}, u32[]{:S(2)}, u32[]{:S(2)}) collective-permute-start(bf16[4,48,896]{2,1,0:T(8,128)(2,1)S(1)} %get-tuple-element.40), channel_id=1, source_target_pairs={{0,8},{1,9},{2,10},{3,11},{4,12},{5,13},{6,14},{7,15},{16,24},{17,... | collective-permute-start | bytes 1032200 | tf_op jit(solution)/shard_map/ppermute | solution.py:37
  127.7 23.2 %collective-permute-start.8 = (bf16[4,48,896]{2,1,0:T(8,128)(2,1)S(1)}, bf16[4,48,896]{2,1,0:T(8,128)(2,1)S(1)}, u32[]{:S(2)}, u32[]{:S(2)}) collective-permute-start(bf16[4,48,896]{2,1,0:T(8,128)(2,1)S(1)} %get-tuple-element.40), channel_id=1, source_target_pairs={{0,24},{1,25},{2,26},{3,27},{4,28},{5,29},{6,30},{7,31},{16,0},{17... | collective-permute-start | bytes 1032200 | tf_op jit(solution)/shard_map/ppermute | solution.py:37
  130.4 25.3 %all-to-all-start.4 = ((bf16[16,32,896]{2,1,0:T(8,128)(2,1)}), bf16[16,32,896]{2,1,0:T(8,128)(2,1)}, u32[]{:S(2)}, u32[]{:S(2)}) async-start(bf16[16,32,896]{2,1,0:T(8,128)(2,1)} %broadcast_in_dim.2), calls=%async_computation.4 | async-start | bytes 1835008 | tf_op jit(solution)/shard_map/all_to_all | solution.py:45
  135.0 19.3 %collective-permute-start.10 = (bf16[4,48,896]{2,1,0:T(8,128)(2,1)S(1)}, bf16[4,48,896]{2,1,0:T(8,128)(2,1)S(1)}, u32[]{:S(2)}, u32[]{:S(2)}) collective-permute-start(bf16[4,48,896]{2,1,0:T(8,128)(2,1)S(1)} %get-tuple-element.40), channel_id=1, source_target_pairs={{0,16},{1,17},{2,18},{3,19},{4,20},{5,21},{6,22},{7,23},{16,8},{17... | collective-permute-start | bytes 1032200 | tf_op jit(solution)/shard_map/ppermute | solution.py:37
  137.9 16.4 %copy-start.4 = (bf16[1,4,48,896]{3,2,1,0:T(8,128)(2,1)S(1)}, bf16[1,4,48,896]{3,2,1,0:T(8,128)(2,1)}, u32[]{:S(2)}) copy-start(bf16[1,4,48,896]{3,2,1,0:T(8,128)(2,1)} %get-tuple-element.39) | copy-start | bytes 1032196
  140.5 13.9 %copy-start.10 = (bf16[4,48,896]{2,1,0:T(8,128)(2,1)}, bf16[4,48,896]{2,1,0:T(8,128)(2,1)S(1)}, u32[]{:S(2)}) copy-start(bf16[4,48,896]{2,1,0:T(8,128)(2,1)S(1)} %collective-permute-done.9) | copy-start | bytes 1032196
  150.9 3.4 %copy-start.11 = (bf16[4,48,896]{2,1,0:T(8,128)(2,1)}, bf16[4,48,896]{2,1,0:T(8,128)(2,1)S(1)}, u32[]{:S(2)}) copy-start(bf16[4,48,896]{2,1,0:T(8,128)(2,1)S(1)} %collective-permute-done.8) | copy-start | bytes 1032196
  156.9 3.0 %copy-start.5 = (bf16[14,32,896]{2,1,0:T(8,128)(2,1)}, bf16[14,32,896]{2,1,0:T(8,128)(2,1)S(1)}, u32[]{:S(2)}) copy-start(bf16[14,32,896]{2,1,0:T(8,128)(2,1)S(1)} %slice.58) | copy-start | bytes 2408452
  156.9 3.0 %slice-start = ((bf16[4,4,88,1152]{3,2,1,0:T(8,128)(2,1)}), bf16[4,4,48,1152]{3,2,1,0:T(8,128)(2,1)S(1)}, s32[]{:S(2)}) async-start(bf16[4,4,88,1152]{3,2,1,0:T(8,128)(2,1)} %fusion), calls=%async_computation.6 | async-start | bytes 3538944 | tf_op jit(solution)/shard_map/slice | solution.py:98
  159.8 2.1 copy-start
  164.0 4.6 %collective-permute-start.17 = (bf16[448,1152]{1,0:T(8,128)(2,1)S(1)}, bf16[448,1152]{1,0:T(8,128)(2,1)S(1)}, u32[]{:S(2)}, u32[]{:S(2)}) collective-permute-start(bf16[448,1152]{1,0:T(8,128)(2,1)S(1)} %slice.82), channel_id=1, source_target_pairs={{0,1},{1,0},{2,3},{3,2},{4,5},{5,4},{6,7},{7,6},{16,17},{17,16},{1... | collective-permute-start | bytes 3096584 | tf_op jit(solution)/shard_map/ppermute | solution.py:37
  170.0 24.3 %collective-permute-start.19 = (bf16[448,1152]{1,0:T(8,128)(2,1)}, bf16[448,1152]{1,0:T(8,128)(2,1)}, u32[]{:S(2)}, u32[]{:S(2)}) collective-permute-start(bf16[448,1152]{1,0:T(8,128)(2,1)} %fusion.12), channel_id=1, source_target_pairs={{0,96},{1,97},{2,98},{3,99},{4,100},{5,101},{6,102},{7,103},{16,11... | collective-permute-start | bytes 3096584 | tf_op jit(solution)/shard_map/ppermute | solution.py:37
  170.6 26.7 %collective-permute-start.18 = (bf16[448,1152]{1,0:T(8,128)(2,1)}, bf16[448,1152]{1,0:T(8,128)(2,1)}, u32[]{:S(2)}, u32[]{:S(2)}) collective-permute-start(bf16[448,1152]{1,0:T(8,128)(2,1)} %fusion.12), channel_id=1, source_target_pairs={{0,32},{1,33},{2,34},{3,35},{4,36},{5,37},{6,38},{7,39},{16,48},{1... | collective-permute-start | bytes 3096584 | tf_op jit(solution)/shard_map/ppermute | solution.py:37
  195.5 12.1 %collective-permute-start.21 = (bf16[224,1152]{1,0:T(8,128)(2,1)S(1)}, bf16[224,1152]{1,0:T(8,128)(2,1)S(1)}, u32[]{:S(2)}, u32[]{:S(2)}) collective-permute-start(bf16[224,1152]{1,0:T(8,128)(2,1)S(1)} %slice.64), channel_id=1, source_target_pairs={{0,96},{1,97},{2,98},{3,99},{4,100},{5,101},{6,102},{7,103},{16,11... | collective-permute-start | bytes 1548296 | tf_op jit(solution)/shard_map/ppermute | solution.py:37
  198.4 13.0 %collective-permute-start.20 = (bf16[224,1152]{1,0:T(8,128)(2,1)S(1)}, bf16[224,1152]{1,0:T(8,128)(2,1)S(1)}, u32[]{:S(2)}, u32[]{:S(2)}) collective-permute-start(bf16[224,1152]{1,0:T(8,128)(2,1)S(1)} %slice.63), channel_id=1, source_target_pairs={{0,32},{1,33},{2,34},{3,35},{4,36},{5,37},{6,38},{7,39},{16,48},{1... | collective-permute-start | bytes 1548296 | tf_op jit(solution)/shard_map/ppermute | solution.py:37
  200.4 11.0 %copy-start.6 = (bf16[14,32,896]{2,1,0:T(8,128)(2,1)S(1)}, bf16[14,32,896]{2,1,0:T(8,128)(2,1)}, u32[]{:S(2)}) copy-start(bf16[14,32,896]{2,1,0:T(8,128)(2,1)} %copy-done.5) | copy-start | bytes 2408452
  213.4 4.7 %collective-permute-start.22 = (bf16[448,1152]{1,0:T(8,128)(2,1)S(1)}, bf16[448,1152]{1,0:T(8,128)(2,1)S(1)}, u32[]{:S(2)}, u32[]{:S(2)}) collective-permute-start(bf16[448,1152]{1,0:T(8,128)(2,1)S(1)} %slice.81), channel_id=1, source_target_pairs={{0,1},{1,0},{2,3},{3,2},{4,5},{5,4},{6,7},{7,6},{16,17},{17,16},{1... | collective-permute-start | bytes 3096584 | tf_op jit(solution)/shard_map/ppermute | solution.py:37
